TPU v7x, 512 devices: a whole 4x8x8 slice. The times are simulated.
512 devices in a mesh: row: 8 (over z), col: 16 (over y_hi, x, core), kpart: 4 (over y_lo).
Axes of the slice: x: 4, y: 8 (y_hi: 2, y_lo: 4; y = y_hi * 4 + y_lo), z: 8, core: 2. Of those that a mesh axis runs over, the one named last changes fastest.
Arguments:
- left_cyclic: float32 [2048, 8192], P(('kpart', 'col'), 'row'), may hold values from -6 to 6
- right_cyclic: float32 [2048, 16384], P(('kpart', 'row'), 'col'), may hold values from -0.125 to 0.125
Outputs:
- product: float32 [8192, 16384], P(('row', 'kpart'), 'col')
All inputs are finite; a program needn't handle non-finite values.
Results may differ from a plain program's by a relative error of at most 0.00007.
Values sent between devices are 32-bit elements; how exact they have to be, the bound alone decides.
No kernel may reach another device: no remote copies, remote signals or barrier semaphores. Data moves between devices by JAX's collectives and lax.ppermute only.
A program may use at most 64 MiB of HBM per device.

v0:
```python
import jax
import jax.numpy as jnp
from jax import lax
from jax.sharding import PartitionSpec as P

NB = 64


def contract(left_part, right_part):
    return lax.dot_general(
        left_part,
        right_part,
        (((0,), (0,)), ((), ())),
        precision=lax.Precision.HIGHEST,
        preferred_element_type=jnp.float32,
    )


def shards(left_cyclic, right_cyclic):
    row_count = lax.axis_size("row")
    column_count = lax.axis_size("col")
    slab_left, local_rows = left_cyclic.shape
    group_left = local_rows // (NB * row_count)
    shaped_left = left_cyclic.reshape(slab_left, row_count, group_left, 1, NB)
    moved_left = lax.all_to_all(shaped_left, "row", split_axis=1, concat_axis=3, tiled=True)
    band_left = moved_left.reshape(slab_left, local_rows)
    left_band = lax.all_gather(band_left, "col", axis=0, tiled=True)
    slab_right, local_cols = right_cyclic.shape
    group_right = local_cols // (NB * column_count)
    shaped_right = right_cyclic.reshape(slab_right, column_count, group_right, 1, NB)
    moved_right = lax.all_to_all(shaped_right, "col", split_axis=1, concat_axis=3, tiled=True)
    band_right = moved_right.reshape(slab_right, local_cols)
    right_band = lax.all_gather(band_right, "row", axis=0, tiled=True)
    return lax.psum_scatter(
        contract(left_band, right_band), "kpart", scatter_dimension=0, tiled=True
    )


def solution(mesh):
    placed = (P(("kpart", "col"), "row"), P(("kpart", "row"), "col"))
    return jax.shard_map(
        shards, mesh=mesh, in_specs=placed, out_specs=P(("row", "kpart"), "col"), check_vma=False
    )
```

profile of v0, /device:TPU:1, one launch (start us, length us, event | category | flops | bytes accessed | tf_op | source)
XLA Modules:
  0.0 246.0 jit_solution(4141008044242358849)
XLA Ops:
  6.5 0.0 all-gather.5.cloned.1.call-start
  6.5 1.1 reshape.19
  7.6 0.2 copy.11
  7.8 0.3 reshape.23
  8.1 0.0 copy-start
  8.2 22.1 %all_to_all.24 = f32[16,1,4096]{2,1,0:T(1,128)S(1)} all-to-all(f32[16,1,4096]{2,1,0:T(1,128)S(1)} %reshape.23), channel_id=1, replica_groups=mesh['row'=8,'col'=16,'kpart'=4] {'col'}, dimensions={0} | all-to-all | bytes 524288 | tf_op jit(solution)/shard_map/all_to_all | solution.py:31
  30.2 0.5 broadcast
  30.8 1.2 reduce.1
  32.0 0.2 reshape.24
  32.3 0.3 copy.8
  32.6 0.9 reshape.20
  33.5 0.0 all-gather.5.cloned.1.call-update
  33.5 0.0 all-gather.3.cloned.1.call-start
  33.5 0.0 copy-done
  33.5 0.2 reshape.17
  33.7 0.1 copy.12
  33.8 0.3 reshape.21
  34.1 17.9 %all_to_all.25 = f32[8,1,4096]{2,1,0:T(1,128)S(1)} all-to-all(f32[8,1,4096]{2,1,0:T(1,128)S(1)} %reshape.21), channel_id=1, replica_groups=mesh['row'=8,'col'=16,'kpart'=4] {'row'}, dimensions={0} | all-to-all | bytes 262144 | tf_op jit(solution)/shard_map/all_to_all | solution.py:25
  52.0 0.9 reduce
  52.9 0.2 reshape.22
  53.2 0.2 copy.6
  53.3 0.8 reshape.18
  54.1 0.0 all-gather.3.cloned.1.call-update
  54.1 0.0 reduce-scatter.2.cloned.1.call-start
  54.2 20.7 %all-gather.5.cloned.1.call-done = f32[512,1024]{1,0:T(8,128)} async-done(((f32[64,1024]{1,0:T(8,128)}), f32[512,1024]{1,0:T(8,128)}) %all-gather.5.cloned.1.call-update) | async-done | bytes 2097168 | tf_op jit(solution)/shard_map/all_gather | solution.py:33
  74.9 72.5 %all-gather.3.cloned.1.call-done = f32[512,1024]{1,0:T(8,128)} async-done(((f32[32,1024]{1,0:T(8,128)}), f32[512,1024]{1,0:T(8,128)}) %all-gather.3.cloned.1.call-update) | async-done | bytes 2097168 | tf_op jit(solution)/shard_map/all_gather | solution.py:27
  147.4 10.2 %fusion = f32[1024,1024]{1,0:T(8,128)} fusion(f32[512,1024]{1,0:T(8,128)} %all-gather.3.cloned.1.call-done, f32[512,1024]{1,0:T(8,128)} %all-gather.5.cloned.1.call-done), kind=kOutput, calls=%fused_computation.3 | convolution fusion | flops 6442450944 | bytes 8388608 | tf_op jit(solution)/shard_map/dot_general | solution.py:10
  157.6 0.0 reduce-scatter.2.cloned.1.call-update
  157.6 81.8 %reduce-scatter.2.cloned.1.call-done = f32[256,1024]{1,0:T(8,128)} async-done(((f32[1024,1024]{1,0:T(8,128)}), f32[256,1024]{1,0:T(8,128)}) %reduce-scatter.2.cloned.1.call-update) | async-done | bytes 1048592 | tf_op jit(solution)/shard_map/reduce_scatter | solution.py:34
  (1 shorter events, 0.0 us)
Async XLA Ops:
  6.5 68.3 %all-gather.5.cloned.1.call-start = ((), (), s32[]{:S(2)}) async-start(), calls=%async_computation.4 | async-start | bytes 2359296 | tf_op jit(solution)/shard_map/all_gather | solution.py:33
  8.1 25.4 %copy-start = (f32[32,1024]{1,0:T(8,128)S(1)}, f32[32,1024]{1,0:T(8,128)}, u32[]{:S(2)}) copy-start(f32[32,1024]{1,0:T(8,128)} %param.2) | copy-start | bytes 393220
  33.5 113.9 %all-gather.3.cloned.1.call-start = ((), (), s32[]{:S(2)}) async-start(), calls=%async_computation.3 | async-start | bytes 2228224 | tf_op jit(solution)/shard_map/all_gather | solution.py:27
  54.1 185.3 %reduce-scatter.2.cloned.1.call-start = ((), (), s32[]{:S(2)}) async-start(), calls=%async_computation.5 | async-start | bytes 5242880 | tf_op jit(solution)/shard_map/reduce_scatter | solution.py:34
Sparse Core Ops, SparseCore 0:
  33.6 41.2 all-gather.4
  78.2 69.1 all-gather.2
  157.8 81.6 reduce-scatter.1
where the time goes:
time: 247 us; the launch traced here: 246 us
  waiting for transfers between devices  175 us (71%)
  blocking collectives  40 us (16%)
  between operations  13.2 us (5%)
  matrix products  10.2 us (4%)
  local copies, waits for them, and re-layouts  5.21 us (2%)
    reduce_scatter x1, waiting for transfers between devices, shards(): lax.psum_scatter(contract(left_band, right_band), 'kpart', scatter_dimens...  81.8 us
    all_gather x1, waiting for transfers between devices, shards(): left_band = lax.all_gather(band_left, 'col', axis=0, tiled=True)  72.5 us
    all_to_all x1, blocking collectives, shards(): lax.all_to_all(shaped_right, 'col', split_axis=1, concat_axis=3, tiled=True)  22.1 us
    all_gather x1, waiting for transfers between devices, shards(): right_band = lax.all_gather(band_right, 'row', axis=0, tiled=True)  20.7 us
    all_to_all x1, blocking collectives, shards(): lax.all_to_all(shaped_left, 'row', split_axis=1, concat_axis=3, tiled=True)  17.9 us
    dot_general x1, matrix products, contract(): lax.dot_general(left_part, right_part, (((0,), (0,)), ((), ())), precisio...  10.2 us
  transfers between devices with their start and end apart: 3, of which 3 were waited for; matrix products, arithmetic and copies ran while one was open for 1% of the time, Pallas kernels for 0%

commit v1 on v0

v1 whole, which is shorter than its diff:
```python
import functools

import jax
import jax.numpy as jnp
from jax import lax
from jax.experimental import pallas as pl
from jax.experimental.pallas import tpu as pltpu
from jax.sharding import Mesh, PartitionSpec as P

F32 = jnp.float32
BF16 = jnp.bfloat16
PLACE = ((0, 2, 1, 3), (1, 3, 2, 0))


def whole(n):
    return [pl.BlockSpec(memory_space=pltpu.VMEM)] * n


def params():
    return pltpu.CompilerParams(vmem_limit_bytes=24 * 1024 * 1024)


def groups(shape, width):
    return lax.broadcasted_iota(jnp.int32, shape, len(shape) - 1) // width


def pick(where, parts):
    out = parts[0]
    for g in range(1, len(parts)):
        out = jnp.where(where == g, parts[g], out)
    return out


def pack_right_kernel(x_ref, out_ref):
    g = groups((16, 128), 32)
    for hx in range(8):
        rolled = []
        for i in range(4):
            tile = x_ref[16 * i : 16 * i + 16, 128 * hx : 128 * hx + 128]
            rolled.append(pltpu.roll(tile, 32 * i, 1) if i else tile)
        for p in range(4):
            msg = pick(g, [rolled[(k - p) % 4] for k in range(4)])
            for a in range(2):
                out_ref[(2 * hx + p // 2) * 4 + 2 * a + p % 2] = msg


def unpack_right_kernel(core, half, in_ref, out_ref):
    g = groups((16, 128), 32)
    core, half = core(), half()
    p = 2 * core + half

    def run(place):
        for l in range(4):
            for t in range(4):
                rolled = []
                for m in range(4):
                    msg = in_ref[(4 * t + m) * 4 + l]
                    rolled.append(pltpu.roll(msg, 32 * place[m], 1) if place[m] else msg)
                for j in range(4):
                    order = [None] * 4
                    for m in range(4):
                        order[(j + place[m]) % 4] = rolled[m]
                    row = pick(g, order)
                    if j:
                        row = pltpu.roll(row, 32 * (4 - j), 1)
                    i = lax.rem(j - p + 4, 4)
                    s = i // 2
                    out_ref[lax.rem(s + core, 2), l, lax.rem(i, 2), :, 128 * t : 128 * t + 128] = row

    for h in range(2):
        pl.when(half == h)(functools.partial(run, PLACE[h]))


def pack_left_kernel(x_ref, out_ref):
    low = groups((16, 128), 64) == 0
    for z in range(8):
        top = x_ref[0:16, 128 * z : 128 * z + 128]
        bottom = x_ref[16:32, 128 * z : 128 * z + 128]
        first = jnp.where(low, top, pltpu.roll(bottom, 64, 1))
        second = jnp.where(low, pltpu.roll(top, 64, 1), bottom)
        for h in range(2):
            for b in range(2):
                out_ref[z * 8 + h * 4 + b] = first
                out_ref[z * 8 + h * 4 + 2 + b] = second


def unpack_left_kernel(in_ref, *refs):
    out_ref = refs[-1]
    low = groups((16, 128), 64) == 0
    for h in range(2):
        for t in range(4):
            rows = []
            for l in range(4):
                even = in_ref[(2 * t) * 8 + h * 4 + l]
                odd = in_ref[(2 * t + 1) * 8 + h * 4 + l]
                rows.append(jnp.where(low, even, pltpu.roll(odd, 64, 1)))
                rows.append(jnp.where(low, pltpu.roll(even, 64, 1), odd))
            block = jnp.concatenate(rows, axis=0).T
            for d in range(4):
                out_ref[d, h, 128 * t : 128 * t + 128, :] = block


def split(x):
    high = x.astype(BF16)
    return high, (x - high.astype(F32)).astype(BF16)


def product(left, right):
    a, c = split(left)
    b, d = split(right)
    dot = functools.partial(jnp.dot, preferred_element_type=F32)
    return dot(a, b) + dot(a, d) + dot(c, b)


def term_kernel(sizes, first, *refs):
    refs = list(refs[1:])
    acc = None if first else refs[-2][...]
    for size in sizes:
        own, other = refs.pop(0), refs.pop(0)
        parts = [refs.pop(0)[...].reshape(256 // size, 512) for _ in range(size)]
        a = jnp.concatenate([own[0], other[0]], axis=1)
        x = product(a, jnp.concatenate(parts, axis=0) if size > 1 else parts[0])
        acc = x if acc is None else acc + x
    refs[-1][...] = acc


def terms(at, own, other, chunks, acc, tiles):
    one = tiles == 1
    tile = (lambda m, at: at[0]) if one else (lambda m, at: m)
    specs, ops = [], []
    for k, chunk in enumerate(chunks):
        left = pl.BlockSpec((1, 256, 128), functools.partial(lambda k, m, at: (at[k + 1], tile(m, at), 0), k))
        specs += [left, left]
        ops += [own, other]
        for part in chunk:
            specs.append(pl.BlockSpec(part.shape, lambda m, at: (0, 0, 0)))
            ops.append(part)
    if acc is not None:
        specs.append(pl.BlockSpec((256, 512), lambda m, at: (tile(m, at), 0)))
        ops.append(acc)
    return pl.pallas_call(
        functools.partial(term_kernel, [len(c) for c in chunks], acc is None),
        grid_spec=pltpu.PrefetchScalarGridSpec(
            num_scalar_prefetch=1,
            grid=(tiles,),
            in_specs=specs,
            out_specs=pl.BlockSpec((256, 512), lambda m, at: (m, 0)),
        ),
        out_shape=jax.ShapeDtypeStruct((256 * tiles, 512), F32),
        compiler_params=params(),
        cost_estimate=pl.CostEstimate(
            flops=6 * 256 * len(chunks) * 512 * 256 * tiles, bytes_accessed=4 * 512 * 512, transcendentals=0
        ),
    )(at, *ops)


def finish_kernel(half, mine_ref, got_ref, out_ref):
    own = (groups((256, 128), 32) % 2) == half()
    for t in range(4):
        mine = mine_ref[:, 128 * t : 128 * t + 128]
        got = got_ref[:, 128 * t : 128 * t + 128]
        out_ref[:, 256 * t : 256 * t + 128] = jnp.where(own, mine, got)
        out_ref[:, 256 * t + 128 : 256 * t + 256] = pltpu.roll(jnp.where(own, got, mine), 96, 1)


def shift(x, axis, by, n):
    return lax.ppermute(x, axis, [(i, (i + by) % n) for i in range(n)])


def core_index():
    return lax.axis_index("c")


def half_index():
    return lax.rem(lax.axis_index("l"), 2)


def call(kernel, shape, *ops, specs=None):
    return pl.pallas_call(
        kernel,
        in_specs=specs or whole(len(ops)),
        out_specs=pl.BlockSpec(memory_space=pltpu.VMEM),
        out_shape=jax.ShapeDtypeStruct(shape, F32),
        compiler_params=params(),
    )(*ops)


def shards(left, right):
    z = lax.axis_index("z")
    b = half_index()
    r = call(pack_right_kernel, (64, 16, 128), right)
    q = call(pack_left_kernel, (64, 16, 128), left)
    r = lax.all_to_all(r, ("h", "x", "c", "l"), 0, 0, tiled=True)
    r = call(functools.partial(unpack_right_kernel, core_index, half_index), (2, 4, 2, 16, 512), r)
    r = r.reshape(2, 128, 512)

    q, r = lax.optimization_barrier((q, r))
    up1, down1 = shift(r, "z", 1, 8), shift(r, "z", -1, 8)
    q = lax.all_to_all(q, ("z", "h", "l"), 0, 0, tiled=True)
    q, up1, down1 = lax.optimization_barrier((q, up1, down1))
    up2, down2 = shift(up1, "z", 1, 8), shift(down1, "z", -1, 8)
    q = call(unpack_left_kernel, (4, 2, 512, 128), q)
    own = lax.all_to_all(q, "x", 0, 0, tiled=True).reshape(8, 512, 128)
    own, up2, down2 = lax.optimization_barrier((own, up2, down2))
    other = lax.ppermute(own, "c", [(0, 1), (1, 0)])
    up3, down3 = shift(up2, "z", 1, 8), shift(down2, "z", -1, 8)
    other, up3, down3 = lax.optimization_barrier((other, up3, down3))

    def at(tile, *steps):
        zs = (z + jnp.array(steps)) % 8
        return jnp.concatenate([jnp.full((1,), tile, jnp.int32), (zs % 4) * 2 + zs // 4]).astype(jnp.int32)

    total = terms(at(0, 0, -1, 1), own, other, [(r,), (up1,), (down1,)], None, 2)
    total = terms(at(0, -2, 2), own, other, [(up2,), (down2,)], total, 2)
    total = terms(at(0, -3, 3), own, other, [(up3,), (down3,)], total, 2)
    up4 = shift(up3[:1], "z", 1, 8)
    down4 = shift(down3[1:], "z", -1, 8)
    total, up4, down4 = lax.optimization_barrier((total, up4, down4))
    last = (up4, down4)
    theirs = terms(at(1 - b, 4), own, other, [last], total, 1)
    got = lax.ppermute(theirs, "l", [(0, 1), (1, 0), (2, 3), (3, 2)])
    mine = terms(at(b, 4), own, other, [last], total, 1)
    return call(functools.partial(finish_kernel, half_index), (256, 1024), mine, got)


def solution(mesh):
    fine = Mesh(mesh.devices.reshape(8, 2, 4, 2, 4), ("z", "h", "x", "c", "l"))
    col = ("h", "x", "c")
    return jax.shard_map(
        shards,
        mesh=fine,
        in_specs=(P(("l",) + col, "z"), P(("l", "z"), col)),
        out_specs=P(("z", "l"), col),
        check_vma=False,
    )
```

time: 247 us -> 162 us (0.66)
  waiting for transfers between devices: 175 us -> 75 us
  starting transfers between devices: 0.09 us -> 61.3 us
  blocking collectives: 40 us -> 0 us
  Pallas kernels: 0 us -> 16.7 us
  between operations: 13.2 us -> 0.32 us
  matrix products: 10.2 us -> 0 us
    all_gather x2 -> x0, waiting for transfers between devices: 93.3 us -> none  [the longest x1 72.5 us: shards(): left_band = lax.all_gather(band_left, 'col', axis=0, tiled=True)]
    reduce_scatter x1 -> x0, waiting for transfers between devices: 81.8 us -> none  [shards(): lax.psum_scatter(contract(left_band, right_band), 'kpart', scatter_dimens...]
    ppermute x0 -> x10, waiting for transfers between devices: none -> 50.4 us  [the longest x8 41.2 us: shift(): return lax.ppermute(x, axis, [(i, (i + by) % n) for i in range(n)])]
    all_to_all x2 -> x0, blocking collectives: 40 us -> none  [the longest x1 22.1 us: shards(): lax.all_to_all(shaped_right, 'col', split_axis=1, concat_axis=3, tiled=True)]
    ppermute x0 -> x10, starting transfers between devices: none -> 32.9 us  [the longest x8 26.6 us: shift(): return lax.ppermute(x, axis, [(i, (i + by) % n) for i in range(n)])]
    all_to_all x0 -> x3, starting transfers between devices: none -> 28.4 us  [the longest x1 13.1 us: shards(): q = lax.all_to_all(q, ('z', 'h', 'l'), 0, 0, tiled=True)]
    all_to_all x0 -> x3, waiting for transfers between devices: none -> 24.5 us  [the longest x1 15.9 us: shards(): r = lax.all_to_all(r, ('h', 'x', 'c', 'l'), 0, 0, tiled=True)]
    pallas_call x0 -> x10, Pallas kernels: none -> 16.7 us  [the longest x5 12.7 us: terms(): pl.pallas_call(functools.partial(term_kernel, [len(c) for c in chunks], a...]
  transfers between devices with their start and end apart: 3 -> 13, of which waited for: 3 -> 8; matrix products, arithmetic and copies ran while one was open for 1% -> 0% of each run, Pallas kernels for 0% -> 7%
where the time goes in v1:
time: 162 us; the launch traced here: 160 us
  waiting for transfers between devices  75 us (46%)
  starting transfers between devices  61.3 us (38%)
  Pallas kernels  16.7 us (10%)
  local copies, waits for them, and re-layouts  6.68 us (4%)
    ppermute x8, waiting for transfers between devices, shift(): return lax.ppermute(x, axis, [(i, (i + by) % n) for i in range(n)])  41.2 us
    ppermute x8, starting transfers between devices, shift(): return lax.ppermute(x, axis, [(i, (i + by) % n) for i in range(n)])  26.6 us
    all_to_all x1, waiting for transfers between devices, shards(): r = lax.all_to_all(r, ('h', 'x', 'c', 'l'), 0, 0, tiled=True)  15.9 us
    all_to_all x1, starting transfers between devices, shards(): q = lax.all_to_all(q, ('z', 'h', 'l'), 0, 0, tiled=True)  13.1 us
    pallas_call x5, Pallas kernels, terms(): pl.pallas_call(functools.partial(term_kernel, [len(c) for c in chunks], a...  12.7 us
    all_to_all x1, starting transfers between devices, shards(): r = lax.all_to_all(r, ('h', 'x', 'c', 'l'), 0, 0, tiled=True)  11.6 us
    ppermute x1, waiting for transfers between devices, shards(): got = lax.ppermute(theirs, 'l', [(0, 1), (1, 0), (2, 3), (3, 2)])  9.2 us
    all_to_all x1, waiting for transfers between devices, shards(): own = lax.all_to_all(q, 'x', 0, 0, tiled=True).reshape(8, 512, 128)  8.61 us
  transfers between devices with their start and end apart: 13, of which 8 were waited for; matrix products, arithmetic and copies ran while one was open for 0% of the time, Pallas kernels for 7%

profile of v1, /device:TPU:1, one launch (start us, length us, event | category | flops | bytes accessed | tf_op | source)
XLA Modules:
  0.0 160.4 jit_solution(17467603721117774831)
XLA Ops:
  0.0 0.0 copy-start.7
  0.0 0.9 copy-done.7
  1.0 0.9 shard_map.74
  1.9 11.6 %all-to-all-start = ((f32[64,16,128]{2,1,0:T(8,128)}), f32[64,16,128]{2,1,0:T(8,128)S(1)}, u32[]{:S(2)}, u32[]{:S(2)}) async-start(f32[64,16,128]{2,1,0:T(8,128)} %shard_map.74), calls=%async_computation | async-start | bytes 1048576 | tf_op jit(solution)/shard_map/all_to_all | solution.py:193
  13.5 0.0 copy-start.8
  13.5 0.9 copy-done.8
  14.4 0.9 shard_map.73
  15.3 15.9 %all-to-all-done.in_ref = f32[64,16,128]{2,1,0:T(8,128)S(1)} async-done(((f32[64,16,128]{2,1,0:T(8,128)}), f32[64,16,128]{2,1,0:T(8,128)S(1)}, u32[]{:S(2)}, u32[]{:S(2)}) %all-to-all-start) | async-done | bytes 524320 | tf_op jit(solution)/shard_map/all_to_all | solution.py:193
  31.2 0.6 shard_map.75
  31.9 13.1 %all-to-all-start.1 = ((f32[64,16,128]{2,1,0:T(8,128)}), f32[64,16,128]{2,1,0:T(8,128)S(1)}, u32[]{:S(2)}, u32[]{:S(2)}) async-start(f32[64,16,128]{2,1,0:T(8,128)} %shard_map.73), calls=%async_computation.1 | async-start | bytes 1048576 | tf_op jit(solution)/shard_map/all_to_all | solution.py:199
  44.9 2.9 %collective-permute-start = (f32[2,128,512]{2,1,0:T(8,128)S(1)}, f32[2,128,512]{2,1,0:T(8,128)S(1)}, u32[]{:S(2)}, u32[]{:S(2)}) collective-permute-start(f32[2,128,512]{2,1,0:T(8,128)S(1)} %bitcast.15), channel_id=1, source_target_pairs={{0,64},{64,128},{128,192},{192,256},{256,320},{320,384},{384,448},... | collective-permute-start | bytes 1572872 | tf_op jit(solution)/shard_map/ppermute | solution.py:167
  47.9 3.6 %collective-permute-start.1 = (f32[2,128,512]{2,1,0:T(8,128)S(1)}, f32[2,128,512]{2,1,0:T(8,128)S(1)}, u32[]{:S(2)}, u32[]{:S(2)}) collective-permute-start(f32[2,128,512]{2,1,0:T(8,128)S(1)} %bitcast.16), channel_id=1, source_target_pairs={{0,448},{64,0},{128,64},{192,128},{256,192},{320,256},{384,320},{4... | collective-permute-start | bytes 1572872 | tf_op jit(solution)/shard_map/ppermute | solution.py:167
  51.4 20.4 %collective-permute-done.refs_6_ = f32[2,128,512]{2,1,0:T(8,128)S(1)} collective-permute-done((f32[2,128,512]{2,1,0:T(8,128)S(1)}, f32[2,128,512]{2,1,0:T(8,128)S(1)}, u32[]{:S(2)}, u32[]{:S(2)}) %collective-permute-start) | collective-permute-done | bytes 524320 | tf_op jit(solution)/shard_map/ppermute | solution.py:167
  71.9 0.0 copy-start.1
  71.9 0.0 collective-permute-done.1.refs_9_
  71.9 0.8 copy-done.1
  72.7 0.0 copy-start.3
  72.7 0.8 copy-done.3
  73.5 0.0 all-to-all-done.1.in_ref
  73.5 0.4 shard_map.76
  73.8 0.0 copy-start
  73.8 1.3 copy-done
  75.2 0.0 copy-start.2
  75.2 0.0 copy-start.11
  75.2 0.0 copy-start.10
  75.2 3.8 %all-to-all-start.2 = ((f32[4,2,512,128]{3,2,1,0:T(8,128)}), f32[4,2,512,128]{3,2,1,0:T(8,128)S(1)}, u32[]{:S(2)}, u32[]{:S(2)}) async-start(f32[4,2,512,128]{3,2,1,0:T(8,128)} %copy-done), calls=%async_computation.2 | async-start | bytes 4194304 | tf_op jit(solution)/shard_map/all_to_all | solution.py:203
  79.0 0.0 copy-done.2
  79.0 1.9 %collective-permute-start.2 = (f32[2,128,512]{2,1,0:T(8,128)S(1)}, f32[2,128,512]{2,1,0:T(8,128)S(1)}, u32[]{:S(2)}, u32[]{:S(2)}) collective-permute-start(f32[2,128,512]{2,1,0:T(8,128)S(1)} %copy-done.2), channel_id=1, source_target_pairs={{0,64},{64,128},{128,192},{192,256},{256,320},{320,384},{384,448},... | collective-permute-start | bytes 1572872 | tf_op jit(solution)/shard_map/ppermute | solution.py:167
  80.9 4.6 %collective-permute-start.3 = (f32[2,128,512]{2,1,0:T(8,128)}, f32[2,128,512]{2,1,0:T(8,128)}, u32[]{:S(2)}, u32[]{:S(2)}) collective-permute-start(f32[2,128,512]{2,1,0:T(8,128)} %copy-done.3), channel_id=1, source_target_pairs={{0,448},{64,0},{128,64},{192,128},{256,192},{320,256},{384,320},{4... | collective-permute-start | bytes 1572872 | tf_op jit(solution)/shard_map/ppermute | solution.py:167
  85.5 9.4 %collective-permute-done.2.refs_3_ = f32[2,128,512]{2,1,0:T(8,128)S(1)} collective-permute-done((f32[2,128,512]{2,1,0:T(8,128)S(1)}, f32[2,128,512]{2,1,0:T(8,128)S(1)}, u32[]{:S(2)}, u32[]{:S(2)}) %collective-permute-start.2) | collective-permute-done | bytes 524320 | tf_op jit(solution)/shard_map/ppermute | solution.py:167
  94.8 0.0 copy-start.5
  94.8 0.8 copy-done.5
  95.6 0.4 collective-permute-done.3.refs_6_
  96.0 8.6 %all-to-all-done.2 = f32[4,2,512,128]{3,2,1,0:T(8,128)S(1)} async-done(((f32[4,2,512,128]{3,2,1,0:T(8,128)}), f32[4,2,512,128]{3,2,1,0:T(8,128)S(1)}, u32[]{:S(2)}, u32[]{:S(2)}) %all-to-all-start.2) | async-done | bytes 2097184 | tf_op jit(solution)/shard_map/all_to_all | solution.py:203
  104.6 3.5 %collective-permute-start.4 = (f32[8,512,128]{2,1,0:T(8,128)S(1)}, f32[8,512,128]{2,1,0:T(8,128)}, u32[]{:S(2)}, u32[]{:S(2)}) collective-permute-start(f32[8,512,128]{2,1,0:T(8,128)S(1)} %bitcast.5), channel_id=1, source_target_pairs={{0,4},{4,0},{1,5},{5,1},{2,6},{6,2},{3,7},{7,3},{8,12},{12,8},{9,1... | collective-permute-start | bytes 6291464 | tf_op jit(solution)/shard_map/ppermute | solution.py:205
  108.2 0.0 copy-done.11
  108.2 0.1 pad_add_fusion.3.refs_0_
  108.3 1.9 %collective-permute-start.5 = (f32[2,128,512]{2,1,0:T(8,128)}, f32[2,128,512]{2,1,0:T(8,128)S(1)}, u32[]{:S(2)}, u32[]{:S(2)}) collective-permute-start(f32[2,128,512]{2,1,0:T(8,128)} %copy-done.5), channel_id=1, source_target_pairs={{0,64},{64,128},{128,192},{192,256},{256,320},{320,384},{384,448},... | collective-permute-start | bytes 1572872 | tf_op jit(solution)/shard_map/ppermute | solution.py:167
  110.2 4.6 %collective-permute-start.6 = (f32[2,128,512]{2,1,0:T(8,128)}, f32[2,128,512]{2,1,0:T(8,128)S(1)}, u32[]{:S(2)}, u32[]{:S(2)}) collective-permute-start(f32[2,128,512]{2,1,0:T(8,128)} %collective-permute-done.3.refs_6_), channel_id=1, source_target_pairs={{0,448},{64,0},{128,64},{192,128},{256,192},{320,256},{384,320},{4... | collective-permute-start | bytes 1572872 | tf_op jit(solution)/shard_map/ppermute | solution.py:167
  114.8 0.0 copy-done.9
  114.8 0.0 copy-done.10
  114.8 0.1 pad_add_fusion.refs_0_
  114.9 0.1 pad_add_fusion.1.refs_0_
  115.0 0.1 pad_add_fusion.4.refs_0_
  115.0 10.1 %collective-permute-done.5.refs_3_ = f32[2,128,512]{2,1,0:T(8,128)S(1)} collective-permute-done((f32[2,128,512]{2,1,0:T(8,128)}, f32[2,128,512]{2,1,0:T(8,128)S(1)}, u32[]{:S(2)}, u32[]{:S(2)}) %collective-permute-start.5) | collective-permute-done | bytes 524320 | tf_op jit(solution)/shard_map/ppermute | solution.py:167
  125.1 1.0 collective-permute-done.6.refs_6_
  126.1 0.0 collective-permute-done.4.refs_2_.refs_5_.refs_8_
  126.1 2.4 %collective-permute-start.7 = (f32[1,128,512]{2,1,0:T(8,128)S(1)}, f32[1,128,512]{2,1,0:T(8,128)S(1)}, u32[]{:S(2)}, u32[]{:S(2)}) collective-permute-start(f32[1,128,512]{2,1,0:T(8,128)S(1)} %slice.6), channel_id=1, source_target_pairs={{0,64},{64,128},{128,192},{192,256},{256,320},{320,384},{384,448},... | collective-permute-start | bytes 786440 | tf_op jit(solution)/shard_map/ppermute | solution.py:167
  128.5 4.8 %collective-permute-start.8 = (f32[1,128,512]{2,1,0:T(8,128)S(1)}, f32[1,128,512]{2,1,0:T(8,128)S(1)}, u32[]{:S(2)}, u32[]{:S(2)}) collective-permute-start(f32[1,128,512]{2,1,0:T(8,128)S(1)} %slice.7), channel_id=1, source_target_pairs={{0,448},{64,0},{128,64},{192,128},{256,192},{320,256},{384,320},{4... | collective-permute-start | bytes 786440 | tf_op jit(solution)/shard_map/ppermute | solution.py:167
  133.3 0.0 copy-start.4
  133.3 1.0 copy-done.4
  134.3 0.0 copy-start.6
  134.3 3.2 %shard_map.77.refs_7_ = f32[512,512]{1,0:T(8,128)S(1)} custom-call(s32[4]{0:T(128)S(1)} %pad_add_fusion.3.refs_0_, f32[8,512,128]{2,1,0:T(8,128)S(1)} %bitcast.6, f32[8,512,128]{2,1,0:T(8,128)} %collective-permute-done.4.refs_2_.refs_5_.refs_8_, f32[2,128,512]{2,1,0:T(8,128)S(1)} %bitcast.17, f32[8,512,128]{2,1,0:T(8,128)S(1)} %bitcast.7, ...), custom_call_target="tpu_custom_call" | custom-call | flops 1207959552 | bytes 1048576 | tf_op jit(solution)/shard_map/pallas_call | solution.py:141
  137.6 0.0 copy-done.6
  137.6 3.0 %shard_map.78.refs_7_ = f32[512,512]{1,0:T(8,128)S(1)} custom-call(s32[3]{0:T(128)S(1)} %pad_add_fusion.refs_0_, f32[8,512,128]{2,1,0:T(8,128)S(1)} %bitcast.9, f32[8,512,128]{2,1,0:T(8,128)} %collective-permute-done.4.refs_2_.refs_5_.refs_8_, f32[2,128,512]{2,1,0:T(8,128)S(1)} %copy-done.6, f32[8,512,128]{2,1,0:T(8,128)S(1)} %bitcast.10, ...), custom_call_target="tpu_custom_call" | custom-call | flops 805306368 | bytes 1048576 | tf_op jit(solution)/shard_map/pallas_call | solution.py:141
  140.6 2.8 %shard_map.79.refs_5_ = f32[512,512]{1,0:T(8,128)S(1)} custom-call(s32[3]{0:T(128)S(1)} %pad_add_fusion.1.refs_0_, f32[8,512,128]{2,1,0:T(8,128)S(1)} %bitcast.11, f32[8,512,128]{2,1,0:T(8,128)} %collective-permute-done.4.refs_2_.refs_5_.refs_8_, f32[2,128,512]{2,1,0:T(8,128)S(1)} %collective-permute-done.5.refs_3_, f32[8,512,128]{2,1,0:T(8,128)S(1)} %bitcast.12, ...), custom_call_target="tpu_custom_call" | custom-call | flops 805306368 | bytes 1048576 | tf_op jit(solution)/shard_map/pallas_call | solution.py:141
  143.4 0.0 collective-permute-done.7.refs_3_
  143.4 0.0 collective-permute-done.8.refs_4_
  143.4 1.8 %shard_map.81 = f32[256,512]{1,0:T(8,128)S(1)} custom-call(s32[2]{0:T(128)S(1)} %pad_add_fusion.4.refs_0_, f32[8,512,128]{2,1,0:T(8,128)S(1)} %bitcast.13, f32[8,512,128]{2,1,0:T(8,128)} %collective-permute-done.4.refs_2_.refs_5_.refs_8_, f32[1,128,512]{2,1,0:T(8,128)S(1)} %collective-permute-done.7.refs_3_, ...), custom_call_target="tpu_custom_call" | custom-call | flops 201326592 | bytes 1048576 | tf_op jit(solution)/shard_map/pallas_call | solution.py:141
  145.2 2.8 %collective-permute-start.9 = (f32[256,512]{1,0:T(8,128)S(1)}, f32[256,512]{1,0:T(8,128)S(1)}, u32[]{:S(2)}, u32[]{:S(2)}) collective-permute-start(f32[256,512]{1,0:T(8,128)S(1)} %shard_map.81), channel_id=1, source_target_pairs={{0,1},{1,0},{2,3},{3,2},{4,5},{5,4},{6,7},{7,6},{8,9},{9,8},{10,11... | collective-permute-start | bytes 1572872 | tf_op jit(solution)/shard_map/ppermute | solution.py:221
  148.0 0.1 pad_add_fusion.2.refs_0_
  148.1 1.8 %shard_map.80.mine_ref = f32[256,512]{1,0:T(8,128)S(1)} custom-call(s32[2]{0:T(128)S(1)} %pad_add_fusion.2.refs_0_, f32[8,512,128]{2,1,0:T(8,128)S(1)} %bitcast.14, f32[8,512,128]{2,1,0:T(8,128)} %collective-permute-done.4.refs_2_.refs_5_.refs_8_, f32[1,128,512]{2,1,0:T(8,128)S(1)} %collective-permute-done.7.refs_3_, ...), custom_call_target="tpu_custom_call" | custom-call | flops 201326592 | bytes 1048576 | tf_op jit(solution)/shard_map/pallas_call | solution.py:141
  150.0 9.2 %collective-permute-done.9.got_ref = f32[256,512]{1,0:T(8,128)S(1)} collective-permute-done((f32[256,512]{1,0:T(8,128)S(1)}, f32[256,512]{1,0:T(8,128)S(1)}, u32[]{:S(2)}, u32[]{:S(2)}) %collective-permute-start.9) | collective-permute-done | bytes 524320 | tf_op jit(solution)/shard_map/ppermute | solution.py:221
  159.2 1.2 shard_map.82
  (5 shorter events, 0.1 us)
Async XLA Ops:
  0.0 0.9 copy-start.7
  1.9 29.4 %all-to-all-start = ((f32[64,16,128]{2,1,0:T(8,128)}), f32[64,16,128]{2,1,0:T(8,128)S(1)}, u32[]{:S(2)}, u32[]{:S(2)}) async-start(f32[64,16,128]{2,1,0:T(8,128)} %shard_map.74), calls=%async_computation | async-start | bytes 1048576 | tf_op jit(solution)/shard_map/all_to_all | solution.py:193
  13.5 0.9 copy-start.8
  31.9 41.6 %all-to-all-start.1 = ((f32[64,16,128]{2,1,0:T(8,128)}), f32[64,16,128]{2,1,0:T(8,128)S(1)}, u32[]{:S(2)}, u32[]{:S(2)}) async-start(f32[64,16,128]{2,1,0:T(8,128)} %shard_map.73), calls=%async_computation.1 | async-start | bytes 1048576 | tf_op jit(solution)/shard_map/all_to_all | solution.py:199
  44.9 26.9 %collective-permute-start = (f32[2,128,512]{2,1,0:T(8,128)S(1)}, f32[2,128,512]{2,1,0:T(8,128)S(1)}, u32[]{:S(2)}, u32[]{:S(2)}) collective-permute-start(f32[2,128,512]{2,1,0:T(8,128)S(1)} %bitcast.15), channel_id=1, source_target_pairs={{0,64},{64,128},{128,192},{192,256},{256,320},{320,384},{384,448},... | collective-permute-start | bytes 1572872 | tf_op jit(solution)/shard_map/ppermute | solution.py:167
  47.9 24.0 %collective-permute-start.1 = (f32[2,128,512]{2,1,0:T(8,128)S(1)}, f32[2,128,512]{2,1,0:T(8,128)S(1)}, u32[]{:S(2)}, u32[]{:S(2)}) collective-permute-start(f32[2,128,512]{2,1,0:T(8,128)S(1)} %bitcast.16), channel_id=1, source_target_pairs={{0,448},{64,0},{128,64},{192,128},{256,192},{320,256},{384,320},{4... | collective-permute-start | bytes 1572872 | tf_op jit(solution)/shard_map/ppermute | solution.py:167
  71.9 0.8 copy-start.1
  72.7 0.8 copy-start.3
  73.8 1.3 copy-start
  75.2 3.8 %copy-start.2 = (f32[2,128,512]{2,1,0:T(8,128)S(1)}, f32[2,128,512]{2,1,0:T(8,128)}, u32[]{:S(2)}) copy-start(f32[2,128,512]{2,1,0:T(8,128)} %copy-done.1) | copy-start | bytes 1572868
  75.2 33.0 %copy-start.11 = (s32[3]{0:T(128)S(1)}, s32[3]{0:T(128)}, u32[]{:S(2)}) copy-start(s32[3]{0:T(128)} %constant.165.clone) | copy-start | bytes 40
  75.2 39.6 %copy-start.9 = (s32[2]{0:T(128)S(1)}, s32[2]{0:T(128)}, u32[]{:S(2)}) copy-start(s32[2]{0:T(128)} %constant.166.clone) | copy-start | bytes 28
  75.2 39.6 %copy-start.10 = (s32[2]{0:T(128)S(1)}, s32[2]{0:T(128)}, u32[]{:S(2)}) copy-start(s32[2]{0:T(128)} %constant.167.clone) | copy-start | bytes 28
  75.2 29.4 %all-to-all-start.2 = ((f32[4,2,512,128]{3,2,1,0:T(8,128)}), f32[4,2,512,128]{3,2,1,0:T(8,128)S(1)}, u32[]{:S(2)}, u32[]{:S(2)}) async-start(f32[4,2,512,128]{3,2,1,0:T(8,128)} %copy-done), calls=%async_computation.2 | async-start | bytes 4194304 | tf_op jit(solution)/shard_map/all_to_all | solution.py:203
  79.0 15.9 %collective-permute-start.2 = (f32[2,128,512]{2,1,0:T(8,128)S(1)}, f32[2,128,512]{2,1,0:T(8,128)S(1)}, u32[]{:S(2)}, u32[]{:S(2)}) collective-permute-start(f32[2,128,512]{2,1,0:T(8,128)S(1)} %copy-done.2), channel_id=1, source_target_pairs={{0,64},{64,128},{128,192},{192,256},{256,320},{320,384},{384,448},... | collective-permute-start | bytes 1572872 | tf_op jit(solution)/shard_map/ppermute | solution.py:167
  80.9 15.1 %collective-permute-start.3 = (f32[2,128,512]{2,1,0:T(8,128)}, f32[2,128,512]{2,1,0:T(8,128)}, u32[]{:S(2)}, u32[]{:S(2)}) collective-permute-start(f32[2,128,512]{2,1,0:T(8,128)} %copy-done.3), channel_id=1, source_target_pairs={{0,448},{64,0},{128,64},{192,128},{256,192},{320,256},{384,320},{4... | collective-permute-start | bytes 1572872 | tf_op jit(solution)/shard_map/ppermute | solution.py:167
  94.8 0.8 copy-start.5
  104.6 21.5 %collective-permute-start.4 = (f32[8,512,128]{2,1,0:T(8,128)S(1)}, f32[8,512,128]{2,1,0:T(8,128)}, u32[]{:S(2)}, u32[]{:S(2)}) collective-permute-start(f32[8,512,128]{2,1,0:T(8,128)S(1)} %bitcast.5), channel_id=1, source_target_pairs={{0,4},{4,0},{1,5},{5,1},{2,6},{6,2},{3,7},{7,3},{8,12},{12,8},{9,1... | collective-permute-start | bytes 6291464 | tf_op jit(solution)/shard_map/ppermute | solution.py:205
  108.3 16.8 %collective-permute-start.5 = (f32[2,128,512]{2,1,0:T(8,128)}, f32[2,128,512]{2,1,0:T(8,128)S(1)}, u32[]{:S(2)}, u32[]{:S(2)}) collective-permute-start(f32[2,128,512]{2,1,0:T(8,128)} %copy-done.5), channel_id=1, source_target_pairs={{0,64},{64,128},{128,192},{192,256},{256,320},{320,384},{384,448},... | collective-permute-start | bytes 1572872 | tf_op jit(solution)/shard_map/ppermute | solution.py:167
  110.2 15.9 %collective-permute-start.6 = (f32[2,128,512]{2,1,0:T(8,128)}, f32[2,128,512]{2,1,0:T(8,128)S(1)}, u32[]{:S(2)}, u32[]{:S(2)}) collective-permute-start(f32[2,128,512]{2,1,0:T(8,128)} %collective-permute-done.3.refs_6_), channel_id=1, source_target_pairs={{0,448},{64,0},{128,64},{192,128},{256,192},{320,256},{384,320},{4... | collective-permute-start | bytes 1572872 | tf_op jit(solution)/shard_map/ppermute | solution.py:167
  126.1 17.3 %collective-permute-start.7 = (f32[1,128,512]{2,1,0:T(8,128)S(1)}, f32[1,128,512]{2,1,0:T(8,128)S(1)}, u32[]{:S(2)}, u32[]{:S(2)}) collective-permute-start(f32[1,128,512]{2,1,0:T(8,128)S(1)} %slice.6), channel_id=1, source_target_pairs={{0,64},{64,128},{128,192},{192,256},{256,320},{320,384},{384,448},... | collective-permute-start | bytes 786440 | tf_op jit(solution)/shard_map/ppermute | solution.py:167
  128.5 14.9 %collective-permute-start.8 = (f32[1,128,512]{2,1,0:T(8,128)S(1)}, f32[1,128,512]{2,1,0:T(8,128)S(1)}, u32[]{:S(2)}, u32[]{:S(2)}) collective-permute-start(f32[1,128,512]{2,1,0:T(8,128)S(1)} %slice.7), channel_id=1, source_target_pairs={{0,448},{64,0},{128,64},{192,128},{256,192},{320,256},{384,320},{4... | collective-permute-start | bytes 786440 | tf_op jit(solution)/shard_map/ppermute | solution.py:167
  133.3 1.0 copy-start.4
  134.3 3.3 %copy-start.6 = (f32[2,128,512]{2,1,0:T(8,128)S(1)}, f32[2,128,512]{2,1,0:T(8,128)}, u32[]{:S(2)}) copy-start(f32[2,128,512]{2,1,0:T(8,128)} %copy-done.5) | copy-start | bytes 1572868
  145.2 13.9 %collective-permute-start.9 = (f32[256,512]{1,0:T(8,128)S(1)}, f32[256,512]{1,0:T(8,128)S(1)}, u32[]{:S(2)}, u32[]{:S(2)}) collective-permute-start(f32[256,512]{1,0:T(8,128)S(1)} %shard_map.81), channel_id=1, source_target_pairs={{0,1},{1,0},{2,3},{3,2},{4,5},{5,4},{6,7},{7,6},{8,9},{9,8},{10,11... | collective-permute-start | bytes 1572872 | tf_op jit(solution)/shard_map/ppermute | solution.py:221

commit v2 on v1

v2 whole, which is shorter than its diff:
```python
import functools

import jax
import jax.numpy as jnp
from jax import lax
from jax.experimental import pallas as pl
from jax.experimental.pallas import tpu as pltpu
from jax.sharding import Mesh, PartitionSpec as P

F32 = jnp.float32
BF16 = jnp.bfloat16
PLACE = ((0, 2, 1, 3), (1, 3, 2, 0))


def params():
    return pltpu.CompilerParams(vmem_limit_bytes=8 * 1024 * 1024)


def groups(shape, width):
    return lax.broadcasted_iota(jnp.int32, shape, len(shape) - 1) // width


def pick(where, parts):
    out = parts[0]
    for g in range(1, len(parts)):
        out = jnp.where(where == g, parts[g], out)
    return out


def pack_right_kernel(x_ref, out_ref):
    g = groups((16, 128), 32)
    for hx in range(8):
        rolled = []
        for i in range(4):
            tile = x_ref[16 * i : 16 * i + 16, 128 * hx : 128 * hx + 128]
            rolled.append(pltpu.roll(tile, 32 * i, 1) if i else tile)
        for p in range(4):
            msg = pick(g, [rolled[(k - p) % 4] for k in range(4)])
            for a in range(2):
                out_ref[(2 * hx + p // 2) * 4 + 2 * a + p % 2] = msg


def unpack_right_kernel(core, half, in_ref, out_ref):
    g = groups((16, 128), 32)
    core, half = core(), half()
    p = 2 * core + half

    def run(place):
        for l in range(4):
            for t in range(4):
                rolled = []
                for m in range(4):
                    msg = in_ref[(4 * t + m) * 4 + l]
                    rolled.append(pltpu.roll(msg, 32 * place[m], 1) if place[m] else msg)
                for j in range(4):
                    order = [None] * 4
                    for m in range(4):
                        order[(j + place[m]) % 4] = rolled[m]
                    row = pick(g, order)
                    if j:
                        row = pltpu.roll(row, 32 * (4 - j), 1)
                    i = lax.rem(j - p + 4, 4)
                    s = i // 2
                    out_ref[lax.rem(s + core, 2), l, lax.rem(i, 2), :, 128 * t : 128 * t + 128] = row

    for h in range(2):
        pl.when(half == h)(functools.partial(run, PLACE[h]))


def pack_left_kernel(x_ref, out_ref):
    low = groups((16, 128), 64) == 0
    for z in range(8):
        top = x_ref[0:16, 128 * z : 128 * z + 128]
        bottom = x_ref[16:32, 128 * z : 128 * z + 128]
        first = jnp.where(low, top, pltpu.roll(bottom, 64, 1))
        second = jnp.where(low, pltpu.roll(top, 64, 1), bottom)
        for h in range(2):
            for b in range(2):
                out_ref[z * 8 + h * 4 + b] = first
                out_ref[z * 8 + h * 4 + 2 + b] = second


def unpack_left_kernel(half, in_ref, theirs_ref, mine_ref):
    low = groups((16, 128), 64) == 0

    def run(outs):
        for h in range(2):
            for t in range(4):
                rows = []
                for l in range(4):
                    even = in_ref[(2 * t) * 8 + h * 4 + l]
                    odd = in_ref[(2 * t + 1) * 8 + h * 4 + l]
                    rows.append(jnp.where(low, even, pltpu.roll(odd, 64, 1)))
                    rows.append(jnp.where(low, pltpu.roll(even, 64, 1), odd))
                block = jnp.concatenate(rows, axis=0).T
                for d in range(4):
                    outs[t // 2][d, h, t % 2 * 128 : t % 2 * 128 + 128, :] = block

    half = half()
    pl.when(half == 0)(functools.partial(run, (mine_ref, theirs_ref)))
    pl.when(half == 1)(functools.partial(run, (theirs_ref, mine_ref)))


def split(x):
    high = x.astype(BF16)
    return high, (x - high.astype(F32)).astype(BF16)


def product(left, right):
    a, c = split(left)
    b, d = split(right)
    dot = functools.partial(jnp.dot, preferred_element_type=F32)
    return dot(a, b) + dot(a, d) + dot(c, b)


def terms_kernel(own_ref, other_ref, right_ref, out_ref, left, right, sems):
    copies = []
    for z in range(8):
        at = z % 4 * 2 + z // 4
        copies.append(
            [
                pltpu.make_async_copy(own_ref.at[at], left.at[z, 0], sems.at[z, 0]),
                pltpu.make_async_copy(other_ref.at[at], left.at[z, 1], sems.at[z, 1]),
                pltpu.make_async_copy(right_ref.at[z], right.at[z], sems.at[z, 2]),
            ]
        )
    for group in copies:
        for copy in group:
            copy.start()
    total = None
    for z, group in enumerate(copies):
        for copy in group:
            copy.wait()
        x = product(jnp.concatenate([left[z, 0], left[z, 1]], axis=1), right[z].reshape(256, 512))
        total = x if total is None else total + x
    out_ref[...] = total


def terms(own, other, right):
    far = pl.BlockSpec(memory_space=pl.ANY)
    return pl.pallas_call(
        terms_kernel,
        in_specs=[far] * 3,
        out_specs=pl.BlockSpec(memory_space=pltpu.VMEM),
        out_shape=jax.ShapeDtypeStruct((256, 512), F32),
        scratch_shapes=[
            pltpu.VMEM((8, 2, 256, 128), F32),
            pltpu.VMEM((8, 2, 128, 512), F32),
            pltpu.SemaphoreType.DMA((8, 3)),
        ],
        compiler_params=pltpu.CompilerParams(vmem_limit_bytes=60 * 1024 * 1024),
        cost_estimate=pl.CostEstimate(flops=6 * 256 * 2048 * 512, bytes_accessed=6 << 20, transcendentals=0),
    )(own, other, right)


def finish_kernel(half, mine_ref, got_ref, out_ref):
    own = (groups((256, 128), 32) % 2) == half()
    for t in range(4):
        mine = mine_ref[:, 128 * t : 128 * t + 128]
        got = got_ref[:, 128 * t : 128 * t + 128]
        out_ref[:, 256 * t : 256 * t + 128] = jnp.where(own, mine, got)
        out_ref[:, 256 * t + 128 : 256 * t + 256] = pltpu.roll(jnp.where(own, got, mine), 96, 1)


def core_index():
    return lax.axis_index("c")


def half_index():
    return lax.rem(lax.axis_index("l"), 2)


def call(kernel, shape, *ops, cost=0):
    spec = pl.BlockSpec(memory_space=pltpu.VMEM)
    outs = len(shape) if isinstance(shape, list) else 0
    out = [jax.ShapeDtypeStruct(s, F32) for s in shape] if outs else jax.ShapeDtypeStruct(shape, F32)
    return pl.pallas_call(
        kernel,
        in_specs=[spec] * len(ops),
        out_specs=[spec] * outs if outs else spec,
        out_shape=out,
        compiler_params=params(),
        cost_estimate=pl.CostEstimate(flops=cost, bytes_accessed=1 << 20, transcendentals=0),
    )(*ops)


def after(x, *others):
    return lax.optimization_barrier((x, *others))[0]


def swap(x, axis, n):
    return lax.ppermute(x, axis, [(i, i ^ 1) for i in range(n)])


def shards(left, right):
    r = call(pack_right_kernel, (64, 16, 128), right)
    q = call(pack_left_kernel, (64, 16, 128), left)
    r = lax.all_to_all(r, ("h", "x", "c", "l"), 0, 0, tiled=True)
    r = call(functools.partial(unpack_right_kernel, core_index, half_index), (2, 4, 2, 16, 512), r)
    r = r.reshape(2, 128, 512)
    w = lax.all_gather(r, "z", axis=0, tiled=False)

    q = lax.all_to_all(after(q, r), ("z", "h", "l"), 0, 0, tiled=True)
    theirs, mine = call(functools.partial(unpack_left_kernel, half_index), [(4, 2, 256, 128)] * 2, q)
    own1 = lax.all_to_all(theirs, "x", 0, 0, tiled=True).reshape(8, 256, 128)
    own2 = lax.all_to_all(after(mine, own1), "x", 0, 0, tiled=True).reshape(8, 256, 128)
    other1 = swap(own1, "c", 2)

    theirs = terms(own1, other1, w)
    got = swap(theirs, "l", 4)
    other2 = swap(own2, "c", 2)
    mine = terms(own2, other2, w)
    return call(functools.partial(finish_kernel, half_index), (256, 1024), mine, got)


def solution(mesh):
    fine = Mesh(mesh.devices.reshape(8, 2, 4, 2, 4), ("z", "h", "x", "c", "l"))
    col = ("h", "x", "c")
    return jax.shard_map(
        shards,
        mesh=fine,
        in_specs=(P(("l",) + col, "z"), P(("l", "z"), col)),
        out_specs=P(("z", "l"), col),
        check_vma=False,
    )
```

time: 162 us -> 137 us (0.85)
  blocking collectives: 0 us -> 73.9 us
  waiting for transfers between devices: 75 us -> 12.1 us
  starting transfers between devices: 61.3 us -> 19.6 us
  between operations: 0.32 us -> 13.5 us
  Pallas kernels: 16.7 us -> 13.3 us
  local copies, waits for them, and re-layouts: 6.68 us -> 3.86 us
    all_to_all x0 -> x3, blocking collectives: none -> 73.9 us  [the longest x1 30 us: shards(): q = lax.all_to_all(after(q, r), ('z', 'h', 'l'), 0, 0, tiled=True)]
    ppermute x10 -> x3, waiting for transfers between devices: 50.4 us -> 6.56 us  [swap(): return lax.ppermute(x, axis, [(i, i ^ 1) for i in range(n)])]
    all_to_all x3 -> x1, starting transfers between devices: 28.4 us -> 3.52 us  [shards(): lax.all_to_all(after(mine, own1), 'x', 0, 0, tiled=True)]
    all_to_all x3 -> x1, waiting for transfers between devices: 24.5 us -> 4.8 us  [shards(): lax.all_to_all(after(mine, own1), 'x', 0, 0, tiled=True)]
    ppermute x10 -> x3, starting transfers between devices: 32.9 us -> 16.1 us  [swap(): return lax.ppermute(x, axis, [(i, i ^ 1) for i in range(n)])]
    pallas_call x10 -> x7, Pallas kernels: 16.7 us -> 13.3 us  [the longest x2 9.11 us: terms(): pl.pallas_call(terms_kernel, in_specs=[far] * 3, out_specs=pl.BlockSpec(m...]
    unnamed x24 -> x12, local copies, waits for them, and re-layouts: 6.64 us -> 3.86 us
  transfers between devices with their start and end apart: 13 -> 5, of which waited for: 8 -> 3; matrix products, arithmetic and copies ran while one was open for 0% -> 0% of each run, Pallas kernels for 7% -> 8%
where the time goes in v2:
time: 137 us; the launch traced here: 136 us
  blocking collectives  73.9 us (54%)
  starting transfers between devices  19.6 us (14%)
  between operations  13.5 us (10%)
  Pallas kernels  13.3 us (10%)
  waiting for transfers between devices  12.1 us (9%)
  local copies, waits for them, and re-layouts  3.86 us (3%)
    all_to_all x1, blocking collectives, shards(): q = lax.all_to_all(after(q, r), ('z', 'h', 'l'), 0, 0, tiled=True)  30 us
    all_to_all x1, blocking collectives, shards(): r = lax.all_to_all(r, ('h', 'x', 'c', 'l'), 0, 0, tiled=True)  29.2 us
    ppermute x3, starting transfers between devices, swap(): return lax.ppermute(x, axis, [(i, i ^ 1) for i in range(n)])  16.1 us
    all_to_all x1, blocking collectives, shards(): own1 = lax.all_to_all(theirs, 'x', 0, 0, tiled=True).reshape(8, 256, 128)  14.7 us
    pallas_call x2, Pallas kernels, terms(): pl.pallas_call(terms_kernel, in_specs=[far] * 3, out_specs=pl.BlockSpec(m...  9.11 us
    ppermute x3, waiting for transfers between devices, swap(): return lax.ppermute(x, axis, [(i, i ^ 1) for i in range(n)])  6.56 us
    all_to_all x1, waiting for transfers between devices, shards(): lax.all_to_all(after(mine, own1), 'x', 0, 0, tiled=True)  4.8 us
    pallas_call x5, Pallas kernels, call(): pl.pallas_call(kernel, in_specs=[spec] * len(ops), out_specs=[spec] * out...  4.19 us
  transfers between devices with their start and end apart: 5, of which 3 were waited for; matrix products, arithmetic and copies ran while one was open for 0% of the time, Pallas kernels for 8%

profile of v2, /device:TPU:1, one launch (start us, length us, event | category | flops | bytes accessed | tf_op | source)
XLA Modules:
  0.0 136.2 jit_solution(4247222767457643361)
XLA Ops:
  6.5 0.0 all-gather.2.cloned.1.call-start
  6.5 0.0 copy-start.1
  6.5 0.9 copy-done.1
  7.5 0.1 shard_map.30
  7.6 29.2 %all_to_all.20.in_ref = f32[64,16,128]{2,1,0:T(8,128)S(1)} all-to-all(f32[64,16,128]{2,1,0:T(8,128)S(1)} %shard_map.30), channel_id=1, replica_groups=mesh['z'=8,'h'=2,'x'=4,'c'=2,'l'=4] {'h','x','c','l'}, dimensions={0} | all-to-all | bytes 1048576 | tf_op jit(solution)/shard_map/all_to_all | solution.py:198
  36.8 1.4 %shard_map.31 = f32[2,4,2,16,512]{4,3,2,1,0:T(8,128)} custom-call(f32[64,16,128]{2,1,0:T(8,128)S(1)} %all_to_all.20.in_ref), custom_call_target="tpu_custom_call" | custom-call | bytes 1048576 | tf_op jit(solution)/shard_map/pallas_call | solution.py:177
  38.2 0.0 all-gather.2.cloned.1.call-update
  38.2 0.0 copy-start.2
  38.2 0.9 copy-done.2
  39.1 0.1 shard_map.28
  39.2 30.0 %all_to_all.21.in_ref = f32[64,16,128]{2,1,0:T(8,128)S(1)} all-to-all(f32[64,16,128]{2,1,0:T(8,128)S(1)} %shard_map.28), channel_id=1, replica_groups=mesh['z'=8,'h'=2,'x'=4,'c'=2,'l'=4] {'z','h','l'}, dimensions={0} | all-to-all | bytes 1048576 | tf_op jit(solution)/shard_map/all_to_all | solution.py:203
  69.2 1.3 shard_map.29
  70.5 14.7 %all_to_all.22 = f32[4,2,256,128]{3,2,1,0:T(8,128)S(1)} all-to-all(f32[4,2,256,128]{3,2,1,0:T(8,128)S(1)} %get-tuple-element.9), channel_id=1, replica_groups=mesh['z'=8,'h'=2,'x'=4,'c'=2,'l'=4] {'x'}, dimensions={0} | all-to-all | bytes 2097152 | tf_op jit(solution)/shard_map/all_to_all | solution.py:205
  85.3 0.0 copy-start.4
  85.3 3.5 %all-to-all-start.2 = ((f32[4,2,256,128]{3,2,1,0:T(8,128)}), f32[4,2,256,128]{3,2,1,0:T(8,128)S(1)}, u32[]{:S(2)}, u32[]{:S(2)}) async-start(f32[4,2,256,128]{3,2,1,0:T(8,128)} %get-tuple-element.10), calls=%async_computation.2 | async-start | bytes 2097152 | tf_op jit(solution)/shard_map/all_to_all | solution.py:206
  88.8 6.0 %collective-permute-start.1 = (f32[8,256,128]{2,1,0:T(8,128)S(1)}, f32[8,256,128]{2,1,0:T(8,128)}, u32[]{:S(2)}, u32[]{:S(2)}) collective-permute-start(f32[8,256,128]{2,1,0:T(8,128)S(1)} %bitcast.5), channel_id=1, source_target_pairs={{0,4},{4,0},{1,5},{5,1},{2,6},{6,2},{3,7},{7,3},{8,12},{12,8},{9,1... | collective-permute-start | bytes 3145736 | tf_op jit(solution)/shard_map/ppermute | solution.py:192
  94.8 4.8 %all-to-all-done.2 = f32[4,2,256,128]{3,2,1,0:T(8,128)S(1)} async-done(((f32[4,2,256,128]{3,2,1,0:T(8,128)}), f32[4,2,256,128]{3,2,1,0:T(8,128)S(1)}, u32[]{:S(2)}, u32[]{:S(2)}) %all-to-all-start.2) | async-done | bytes 1048608 | tf_op jit(solution)/shard_map/all_to_all | solution.py:206
  99.6 0.0 copy-start.3
  99.6 7.1 %collective-permute-start = (f32[8,256,128]{2,1,0:T(8,128)S(1)}, f32[8,256,128]{2,1,0:T(8,128)S(1)}, u32[]{:S(2)}, u32[]{:S(2)}) collective-permute-start(f32[8,256,128]{2,1,0:T(8,128)S(1)} %bitcast.3), channel_id=1, source_target_pairs={{0,4},{4,0},{1,5},{5,1},{2,6},{6,2},{3,7},{7,3},{8,12},{12,8},{9,1... | collective-permute-start | bytes 3145736 | tf_op jit(solution)/shard_map/ppermute | solution.py:192
  106.7 0.0 collective-permute-done.1.other_ref
  106.7 0.7 all-gather.2.cloned.1.call-done.right_ref
  107.4 0.0 copy-done.4
  107.4 4.5 %shard_map.33 = f32[256,512]{1,0:T(8,128)} custom-call(f32[8,256,128]{2,1,0:T(8,128)} %bitcast.6, f32[8,256,128]{2,1,0:T(8,128)} %collective-permute-done.1.other_ref, f32[8,2,128,512]{3,2,1,0:T(8,128)} %all-gather.2.cloned.1.call-done.right_ref), custom_call_target="tpu_custom_call" | custom-call | flops 1610612736 | bytes 6291456 | tf_op jit(solution)/shard_map/pallas_call | solution.py:141
  112.0 3.0 %collective-permute-start.2 = (f32[256,512]{1,0:T(8,128)}, f32[256,512]{1,0:T(8,128)S(1)}, u32[]{:S(2)}, u32[]{:S(2)}) collective-permute-start(f32[256,512]{1,0:T(8,128)} %shard_map.33), channel_id=1, source_target_pairs={{0,1},{1,0},{2,3},{3,2},{4,5},{5,4},{6,7},{7,6},{8,9},{9,8},{10,11... | collective-permute-start | bytes 1572872 | tf_op jit(solution)/shard_map/ppermute | solution.py:192
  115.0 0.0 collective-permute-done.other_ref
  115.0 0.0 copy-done.3
  115.0 0.0 copy-start.5
  115.0 1.0 copy-done.5
  116.0 4.6 %shard_map.32.mine_ref = f32[256,512]{1,0:T(8,128)} custom-call(f32[8,256,128]{2,1,0:T(8,128)} %bitcast.4, f32[8,256,128]{2,1,0:T(8,128)} %copy-done.5, f32[8,2,128,512]{3,2,1,0:T(8,128)} %all-gather.2.cloned.1.call-done.right_ref), custom_call_target="tpu_custom_call" | custom-call | flops 1610612736 | bytes 6291456 | tf_op jit(solution)/shard_map/pallas_call | solution.py:141
  120.6 6.6 %collective-permute-done.2.got_ref = f32[256,512]{1,0:T(8,128)S(1)} collective-permute-done((f32[256,512]{1,0:T(8,128)}, f32[256,512]{1,0:T(8,128)S(1)}, u32[]{:S(2)}, u32[]{:S(2)}) %collective-permute-start.2) | collective-permute-done | bytes 524320 | tf_op jit(solution)/shard_map/ppermute | solution.py:192
  127.1 0.0 copy-start
  127.1 1.0 copy-done
  128.2 1.2 shard_map.34
Async XLA Ops:
  6.5 100.9 %all-gather.2.cloned.1.call-start = ((), (), s32[]{:S(2)}) async-start(), calls=%async_computation.4 | async-start | bytes 4718592 | tf_op jit(solution)/shard_map/all_gather | solution.py:201
  6.5 0.9 copy-start.1
  38.2 0.9 copy-start.2
  85.3 22.2 %copy-start.4 = (f32[4,2,256,128]{3,2,1,0:T(8,128)}, f32[4,2,256,128]{3,2,1,0:T(8,128)S(1)}, u32[]{:S(2)}) copy-start(f32[4,2,256,128]{3,2,1,0:T(8,128)S(1)} %all_to_all.22) | copy-start | bytes 3145732
  85.3 14.3 %all-to-all-start.2 = ((f32[4,2,256,128]{3,2,1,0:T(8,128)}), f32[4,2,256,128]{3,2,1,0:T(8,128)S(1)}, u32[]{:S(2)}, u32[]{:S(2)}) async-start(f32[4,2,256,128]{3,2,1,0:T(8,128)} %get-tuple-element.10), calls=%async_computation.2 | async-start | bytes 2097152 | tf_op jit(solution)/shard_map/all_to_all | solution.py:206
  88.8 17.9 %collective-permute-start.1 = (f32[8,256,128]{2,1,0:T(8,128)S(1)}, f32[8,256,128]{2,1,0:T(8,128)}, u32[]{:S(2)}, u32[]{:S(2)}) collective-permute-start(f32[8,256,128]{2,1,0:T(8,128)S(1)} %bitcast.5), channel_id=1, source_target_pairs={{0,4},{4,0},{1,5},{5,1},{2,6},{6,2},{3,7},{7,3},{8,12},{12,8},{9,1... | collective-permute-start | bytes 3145736 | tf_op jit(solution)/shard_map/ppermute | solution.py:192
  99.6 15.4 %copy-start.3 = (f32[4,2,256,128]{3,2,1,0:T(8,128)}, f32[4,2,256,128]{3,2,1,0:T(8,128)S(1)}, u32[]{:S(2)}) copy-start(f32[4,2,256,128]{3,2,1,0:T(8,128)S(1)} %all-to-all-done.2) | copy-start | bytes 3145732
  99.6 15.4 %collective-permute-start = (f32[8,256,128]{2,1,0:T(8,128)S(1)}, f32[8,256,128]{2,1,0:T(8,128)S(1)}, u32[]{:S(2)}, u32[]{:S(2)}) collective-permute-start(f32[8,256,128]{2,1,0:T(8,128)S(1)} %bitcast.3), channel_id=1, source_target_pairs={{0,4},{4,0},{1,5},{5,1},{2,6},{6,2},{3,7},{7,3},{8,12},{12,8},{9,1... | collective-permute-start | bytes 3145736 | tf_op jit(solution)/shard_map/ppermute | solution.py:192
  112.0 15.1 %collective-permute-start.2 = (f32[256,512]{1,0:T(8,128)}, f32[256,512]{1,0:T(8,128)S(1)}, u32[]{:S(2)}, u32[]{:S(2)}) collective-permute-start(f32[256,512]{1,0:T(8,128)} %shard_map.33), channel_id=1, source_target_pairs={{0,1},{1,0},{2,3},{3,2},{4,5},{5,4},{6,7},{7,6},{8,9},{9,8},{10,11... | collective-permute-start | bytes 1572872 | tf_op jit(solution)/shard_map/ppermute | solution.py:192
  115.0 1.0 copy-start.5
  127.1 1.0 copy-start
Sparse Core Ops, SparseCore 0:
  38.3 69.0 all-gather.1

commit v3 on v2

--- a/solution.py
+++ b/solution.py
@@ -12,8 +12,8 @@
 PLACE = ((0, 2, 1, 3), (1, 3, 2, 0))
 
 
-def params():
-    return pltpu.CompilerParams(vmem_limit_bytes=8 * 1024 * 1024)
+def params(limit=8):
+    return pltpu.CompilerParams(vmem_limit_bytes=limit * 1024 * 1024)
 
 
 def groups(shape, width):
@@ -136,7 +136,7 @@
     out_ref[...] = total
 
 
-def terms(own, other, right):
+def terms(limit, own, other, right):
     far = pl.BlockSpec(memory_space=pl.ANY)
     return pl.pallas_call(
         terms_kernel,
@@ -148,7 +148,7 @@
             pltpu.VMEM((8, 2, 128, 512), F32),
             pltpu.SemaphoreType.DMA((8, 3)),
         ],
-        compiler_params=pltpu.CompilerParams(vmem_limit_bytes=60 * 1024 * 1024),
+        compiler_params=params(limit),
         cost_estimate=pl.CostEstimate(flops=6 * 256 * 2048 * 512, bytes_accessed=6 << 20, transcendentals=0),
     )(own, other, right)
 
@@ -206,10 +206,10 @@
     own2 = lax.all_to_all(after(mine, own1), "x", 0, 0, tiled=True).reshape(8, 256, 128)
     other1 = swap(own1, "c", 2)
 
-    theirs = terms(own1, other1, w)
+    theirs = terms(60, own1, other1, w)
     got = swap(theirs, "l", 4)
     other2 = swap(own2, "c", 2)
-    mine = terms(own2, other2, w)
+    mine = terms(20, own2, other2, w)
     return call(functools.partial(finish_kernel, half_index), (256, 1024), mine, got)
 
 

time: 137 us -> 136 us (level)
  waiting for transfers between devices: 12.1 us -> 9.91 us
    ppermute x3, waiting for transfers between devices: 6.56 us -> 4.4 us  [swap(): return lax.ppermute(x, axis, [(i, i ^ 1) for i in range(n)])]
    unnamed x12 -> x8, local copies, waits for them, and re-layouts: 3.86 us -> 4.03 us
where the time goes in v3:
time: 136 us; the launch traced here: 135 us
  blocking collectives  73.9 us (54%)
  starting transfers between devices  19.6 us (14%)
  Pallas kernels  14.2 us (10%)
  between operations  13.5 us (10%)
  waiting for transfers between devices  9.91 us (7%)
  local copies, waits for them, and re-layouts  4.03 us (3%)
    all_to_all x1, blocking collectives, shards(): q = lax.all_to_all(after(q, r), ('z', 'h', 'l'), 0, 0, tiled=True)  30 us
    all_to_all x1, blocking collectives, shards(): r = lax.all_to_all(r, ('h', 'x', 'c', 'l'), 0, 0, tiled=True)  29.2 us
    ppermute x3, starting transfers between devices, swap(): return lax.ppermute(x, axis, [(i, i ^ 1) for i in range(n)])  16.1 us
    all_to_all x1, blocking collectives, shards(): own1 = lax.all_to_all(theirs, 'x', 0, 0, tiled=True).reshape(8, 256, 128)  14.7 us
    pallas_call x2, Pallas kernels, terms(): pl.pallas_call(terms_kernel, in_specs=[far] * 3, out_specs=pl.BlockSpec(m...  10.1 us
    all_to_all x1, waiting for transfers between devices, shards(): lax.all_to_all(after(mine, own1), 'x', 0, 0, tiled=True)  4.8 us
    ppermute x3, waiting for transfers between devices, swap(): return lax.ppermute(x, axis, [(i, i ^ 1) for i in range(n)])  4.4 us
    pallas_call x5, Pallas kernels, call(): pl.pallas_call(kernel, in_specs=[spec] * len(ops), out_specs=[spec] * out...  4.19 us
  transfers between devices with their start and end apart: 5, of which 3 were waited for; matrix products, arithmetic and copies ran while one was open for 0% of the time, Pallas kernels for 8%

profile of v3, /device:TPU:1, one launch (start us, length us, event | category | flops | bytes accessed | tf_op | source)
XLA Modules:
  0.0 135.2 jit_solution(9037568609460079844)
XLA Ops:
  6.5 0.0 all-gather.2.cloned.1.call-start
  6.5 0.0 copy-start.1
  6.5 0.9 copy-done.1
  7.5 0.1 shard_map.30
  7.6 29.2 %all_to_all.20.in_ref = f32[64,16,128]{2,1,0:T(8,128)S(1)} all-to-all(f32[64,16,128]{2,1,0:T(8,128)S(1)} %shard_map.30), channel_id=1, replica_groups=mesh['z'=8,'h'=2,'x'=4,'c'=2,'l'=4] {'h','x','c','l'}, dimensions={0} | all-to-all | bytes 1048576 | tf_op jit(solution)/shard_map/all_to_all | solution.py:198
  36.8 1.4 %shard_map.31 = f32[2,4,2,16,512]{4,3,2,1,0:T(8,128)} custom-call(f32[64,16,128]{2,1,0:T(8,128)S(1)} %all_to_all.20.in_ref), custom_call_target="tpu_custom_call" | custom-call | bytes 1048576 | tf_op jit(solution)/shard_map/pallas_call | solution.py:177
  38.2 0.0 all-gather.2.cloned.1.call-update
  38.2 0.0 copy-start.2
  38.2 0.9 copy-done.2
  39.1 0.1 shard_map.28
  39.2 30.0 %all_to_all.21.in_ref = f32[64,16,128]{2,1,0:T(8,128)S(1)} all-to-all(f32[64,16,128]{2,1,0:T(8,128)S(1)} %shard_map.28), channel_id=1, replica_groups=mesh['z'=8,'h'=2,'x'=4,'c'=2,'l'=4] {'z','h','l'}, dimensions={0} | all-to-all | bytes 1048576 | tf_op jit(solution)/shard_map/all_to_all | solution.py:203
  69.2 1.3 shard_map.29
  70.5 14.7 %all_to_all.22 = f32[4,2,256,128]{3,2,1,0:T(8,128)S(1)} all-to-all(f32[4,2,256,128]{3,2,1,0:T(8,128)S(1)} %get-tuple-element.9), channel_id=1, replica_groups=mesh['z'=8,'h'=2,'x'=4,'c'=2,'l'=4] {'x'}, dimensions={0} | all-to-all | bytes 2097152 | tf_op jit(solution)/shard_map/all_to_all | solution.py:205
  85.3 0.0 copy-start.3
  85.3 3.5 %all-to-all-start.2 = ((f32[4,2,256,128]{3,2,1,0:T(8,128)}), f32[4,2,256,128]{3,2,1,0:T(8,128)S(1)}, u32[]{:S(2)}, u32[]{:S(2)}) async-start(f32[4,2,256,128]{3,2,1,0:T(8,128)} %get-tuple-element.10), calls=%async_computation.2 | async-start | bytes 2097152 | tf_op jit(solution)/shard_map/all_to_all | solution.py:206
  88.8 6.0 %collective-permute-start.1 = (f32[8,256,128]{2,1,0:T(8,128)S(1)}, f32[8,256,128]{2,1,0:T(8,128)}, u32[]{:S(2)}, u32[]{:S(2)}) collective-permute-start(f32[8,256,128]{2,1,0:T(8,128)S(1)} %bitcast.5), channel_id=1, source_target_pairs={{0,4},{4,0},{1,5},{5,1},{2,6},{6,2},{3,7},{7,3},{8,12},{12,8},{9,1... | collective-permute-start | bytes 3145736 | tf_op jit(solution)/shard_map/ppermute | solution.py:192
  94.8 4.8 %all-to-all-done.2 = f32[4,2,256,128]{3,2,1,0:T(8,128)S(1)} async-done(((f32[4,2,256,128]{3,2,1,0:T(8,128)}), f32[4,2,256,128]{3,2,1,0:T(8,128)S(1)}, u32[]{:S(2)}, u32[]{:S(2)}) %all-to-all-start.2) | async-done | bytes 1048608 | tf_op jit(solution)/shard_map/all_to_all | solution.py:206
  99.6 7.1 %collective-permute-start = (f32[8,256,128]{2,1,0:T(8,128)S(1)}, f32[8,256,128]{2,1,0:T(8,128)S(1)}, u32[]{:S(2)}, u32[]{:S(2)}) collective-permute-start(f32[8,256,128]{2,1,0:T(8,128)S(1)} %bitcast.3), channel_id=1, source_target_pairs={{0,4},{4,0},{1,5},{5,1},{2,6},{6,2},{3,7},{7,3},{8,12},{12,8},{9,1... | collective-permute-start | bytes 3145736 | tf_op jit(solution)/shard_map/ppermute | solution.py:192
  106.7 0.0 collective-permute-done.1.other_ref
  106.7 0.7 all-gather.2.cloned.1.call-done.right_ref
  107.4 0.0 copy-done.3
  107.4 4.5 %shard_map.33 = f32[256,512]{1,0:T(8,128)} custom-call(f32[8,256,128]{2,1,0:T(8,128)} %bitcast.6, f32[8,256,128]{2,1,0:T(8,128)} %collective-permute-done.1.other_ref, f32[8,2,128,512]{3,2,1,0:T(8,128)} %all-gather.2.cloned.1.call-done.right_ref), custom_call_target="tpu_custom_call" | custom-call | flops 1610612736 | bytes 6291456 | tf_op jit(solution)/shard_map/pallas_call | solution.py:141
  112.0 3.0 %collective-permute-start.2 = (f32[256,512]{1,0:T(8,128)}, f32[256,512]{1,0:T(8,128)S(1)}, u32[]{:S(2)}, u32[]{:S(2)}) collective-permute-start(f32[256,512]{1,0:T(8,128)} %shard_map.33), channel_id=1, source_target_pairs={{0,1},{1,0},{2,3},{3,2},{4,5},{5,4},{6,7},{7,6},{8,9},{9,8},{10,11... | collective-permute-start | bytes 1572872 | tf_op jit(solution)/shard_map/ppermute | solution.py:192
  115.0 0.0 collective-permute-done.other_ref
  115.0 0.0 copy-start
  115.0 2.2 %copy-done = f32[8,2,128,512]{3,2,1,0:T(8,128)S(1)} copy-done((f32[8,2,128,512]{3,2,1,0:T(8,128)S(1)}, f32[8,2,128,512]{3,2,1,0:T(8,128)}, u32[]{:S(2)}) %copy-start) | copy-done | bytes 4194328
  117.2 5.5 %shard_map.32.mine_ref = f32[256,512]{1,0:T(8,128)S(1)} custom-call(f32[8,256,128]{2,1,0:T(8,128)S(1)} %bitcast.4, f32[8,256,128]{2,1,0:T(8,128)S(1)} %collective-permute-done.other_ref, f32[8,2,128,512]{3,2,1,0:T(8,128)S(1)} %copy-done), custom_call_target="tpu_custom_call" | custom-call | flops 1610612736 | bytes 6291456 | tf_op jit(solution)/shard_map/pallas_call | solution.py:141
  122.7 4.4 %collective-permute-done.2.got_ref = f32[256,512]{1,0:T(8,128)S(1)} collective-permute-done((f32[256,512]{1,0:T(8,128)}, f32[256,512]{1,0:T(8,128)S(1)}, u32[]{:S(2)}, u32[]{:S(2)}) %collective-permute-start.2) | collective-permute-done | bytes 524320 | tf_op jit(solution)/shard_map/ppermute | solution.py:192
  127.1 1.2 shard_map.34
Async XLA Ops:
  6.5 100.9 %all-gather.2.cloned.1.call-start = ((), (), s32[]{:S(2)}) async-start(), calls=%async_computation.4 | async-start | bytes 4718592 | tf_op jit(solution)/shard_map/all_gather | solution.py:201
  6.5 0.9 copy-start.1
  38.2 0.9 copy-start.2
  85.3 22.2 %copy-start.3 = (f32[4,2,256,128]{3,2,1,0:T(8,128)}, f32[4,2,256,128]{3,2,1,0:T(8,128)S(1)}, u32[]{:S(2)}) copy-start(f32[4,2,256,128]{3,2,1,0:T(8,128)S(1)} %all_to_all.22) | copy-start | bytes 3145732
  85.3 14.3 %all-to-all-start.2 = ((f32[4,2,256,128]{3,2,1,0:T(8,128)}), f32[4,2,256,128]{3,2,1,0:T(8,128)S(1)}, u32[]{:S(2)}, u32[]{:S(2)}) async-start(f32[4,2,256,128]{3,2,1,0:T(8,128)} %get-tuple-element.10), calls=%async_computation.2 | async-start | bytes 2097152 | tf_op jit(solution)/shard_map/all_to_all | solution.py:206
  88.8 17.9 %collective-permute-start.1 = (f32[8,256,128]{2,1,0:T(8,128)S(1)}, f32[8,256,128]{2,1,0:T(8,128)}, u32[]{:S(2)}, u32[]{:S(2)}) collective-permute-start(f32[8,256,128]{2,1,0:T(8,128)S(1)} %bitcast.5), channel_id=1, source_target_pairs={{0,4},{4,0},{1,5},{5,1},{2,6},{6,2},{3,7},{7,3},{8,12},{12,8},{9,1... | collective-permute-start | bytes 3145736 | tf_op jit(solution)/shard_map/ppermute | solution.py:192
  99.6 15.4 %collective-permute-start = (f32[8,256,128]{2,1,0:T(8,128)S(1)}, f32[8,256,128]{2,1,0:T(8,128)S(1)}, u32[]{:S(2)}, u32[]{:S(2)}) collective-permute-start(f32[8,256,128]{2,1,0:T(8,128)S(1)} %bitcast.3), channel_id=1, source_target_pairs={{0,4},{4,0},{1,5},{5,1},{2,6},{6,2},{3,7},{7,3},{8,12},{12,8},{9,1... | collective-permute-start | bytes 3145736 | tf_op jit(solution)/shard_map/ppermute | solution.py:192
  112.0 15.1 %collective-permute-start.2 = (f32[256,512]{1,0:T(8,128)}, f32[256,512]{1,0:T(8,128)S(1)}, u32[]{:S(2)}, u32[]{:S(2)}) collective-permute-start(f32[256,512]{1,0:T(8,128)} %shard_map.33), channel_id=1, source_target_pairs={{0,1},{1,0},{2,3},{3,2},{4,5},{5,4},{6,7},{7,6},{8,9},{9,8},{10,11... | collective-permute-start | bytes 1572872 | tf_op jit(solution)/shard_map/ppermute | solution.py:192
  115.0 2.2 %copy-start = (f32[8,2,128,512]{3,2,1,0:T(8,128)S(1)}, f32[8,2,128,512]{3,2,1,0:T(8,128)}, u32[]{:S(2)}) copy-start(f32[8,2,128,512]{3,2,1,0:T(8,128)} %all-gather.2.cloned.1.call-done.right_ref) | copy-start | bytes 12582916
Sparse Core Ops, SparseCore 0:
  38.3 69.0 all-gather.1

commit v4 on v3

--- a/solution.py
+++ b/solution.py
@@ -67,17 +67,16 @@
         pl.when(half == h)(functools.partial(run, PLACE[h]))
 
 
-def pack_left_kernel(x_ref, out_ref):
+def pack_left_kernel(in_ref, out_ref):
     low = groups((16, 128), 64) == 0
     for z in range(8):
-        top = x_ref[0:16, 128 * z : 128 * z + 128]
-        bottom = x_ref[16:32, 128 * z : 128 * z + 128]
+        top, bottom = in_ref[z, 0:16], in_ref[z, 16:32]
         first = jnp.where(low, top, pltpu.roll(bottom, 64, 1))
         second = jnp.where(low, pltpu.roll(top, 64, 1), bottom)
         for h in range(2):
             for b in range(2):
-                out_ref[z * 8 + h * 4 + b] = first
-                out_ref[z * 8 + h * 4 + 2 + b] = second
+                out_ref[h * 4 + b, z] = first
+                out_ref[h * 4 + 2 + b, z] = second
 
 
 def unpack_left_kernel(half, in_ref, theirs_ref, mine_ref):
@@ -88,13 +87,17 @@
             for t in range(4):
                 rows = []
                 for l in range(4):
-                    even = in_ref[(2 * t) * 8 + h * 4 + l]
-                    odd = in_ref[(2 * t + 1) * 8 + h * 4 + l]
+                    even = in_ref[h * 4 + l, 2 * t]
+                    odd = in_ref[h * 4 + l, 2 * t + 1]
                     rows.append(jnp.where(low, even, pltpu.roll(odd, 64, 1)))
                     rows.append(jnp.where(low, pltpu.roll(even, 64, 1), odd))
                 block = jnp.concatenate(rows, axis=0).T
-                for d in range(4):
-                    outs[t // 2][d, h, t % 2 * 128 : t % 2 * 128 + 128, :] = block
+                out, rows = outs[t // 2], slice(t % 2 * 128, t % 2 * 128 + 128)
+                if len(out.shape) == 3:
+                    out[h, rows] = block
+                else:
+                    for d in range(4):
+                        out[d, h, rows] = block
 
     half = half()
     pl.when(half == 0)(functools.partial(run, (mine_ref, theirs_ref)))
@@ -113,17 +116,16 @@
     return dot(a, b) + dot(a, d) + dot(c, b)
 
 
-def terms_kernel(own_ref, other_ref, right_ref, out_ref, left, right, sems):
+def terms_kernel(*refs):
+    own_ref, *other_refs, right_ref, out_ref, left, right, sems = refs
+    each = 4 // len(other_refs)
     copies = []
     for z in range(8):
-        at = z % 4 * 2 + z // 4
-        copies.append(
-            [
-                pltpu.make_async_copy(own_ref.at[at], left.at[z, 0], sems.at[z, 0]),
-                pltpu.make_async_copy(other_ref.at[at], left.at[z, 1], sems.at[z, 1]),
-                pltpu.make_async_copy(right_ref.at[z], right.at[z], sems.at[z, 2]),
-            ]
-        )
+        x, h = z % 4, z // 4
+        group = [pltpu.make_async_copy(right_ref.at[z], right.at[z], sems.at[z, 2])]
+        group.append(pltpu.make_async_copy(own_ref.at[x, h], left.at[z, 0], sems.at[z, 0]))
+        group.append(pltpu.make_async_copy(other_refs[x // each].at[x % each, h], left.at[z, 1], sems.at[z, 1]))
+        copies.append(group)
     for group in copies:
         for copy in group:
             copy.start()
@@ -136,11 +138,11 @@
     out_ref[...] = total
 
 
-def terms(limit, own, other, right):
+def terms(limit, right, *left):
     far = pl.BlockSpec(memory_space=pl.ANY)
     return pl.pallas_call(
         terms_kernel,
-        in_specs=[far] * 3,
+        in_specs=[far] * (1 + len(left)),
         out_specs=pl.BlockSpec(memory_space=pltpu.VMEM),
         out_shape=jax.ShapeDtypeStruct((256, 512), F32),
         scratch_shapes=[
@@ -150,7 +152,7 @@
         ],
         compiler_params=params(limit),
         cost_estimate=pl.CostEstimate(flops=6 * 256 * 2048 * 512, bytes_accessed=6 << 20, transcendentals=0),
-    )(own, other, right)
+    )(*left, right)
 
 
 def finish_kernel(half, mine_ref, got_ref, out_ref):
@@ -194,22 +196,23 @@
 
 def shards(left, right):
     r = call(pack_right_kernel, (64, 16, 128), right)
-    q = call(pack_left_kernel, (64, 16, 128), left)
+    q = left.reshape(32, 8, 128).transpose(1, 0, 2)
     r = lax.all_to_all(r, ("h", "x", "c", "l"), 0, 0, tiled=True)
     r = call(functools.partial(unpack_right_kernel, core_index, half_index), (2, 4, 2, 16, 512), r)
     r = r.reshape(2, 128, 512)
     w = lax.all_gather(r, "z", axis=0, tiled=False)
 
-    q = lax.all_to_all(after(q, r), ("z", "h", "l"), 0, 0, tiled=True)
+    q = lax.all_to_all(after(q, r), "z", 0, 0, tiled=True)
+    q = call(pack_left_kernel, (8, 8, 16, 128), q)
+    q = lax.all_to_all(q, ("h", "l"), 0, 0, tiled=True)
     theirs, mine = call(functools.partial(unpack_left_kernel, half_index), [(4, 2, 256, 128)] * 2, q)
-    own1 = lax.all_to_all(theirs, "x", 0, 0, tiled=True).reshape(8, 256, 128)
-    own2 = lax.all_to_all(after(mine, own1), "x", 0, 0, tiled=True).reshape(8, 256, 128)
-    other1 = swap(own1, "c", 2)
-
-    theirs = terms(60, own1, other1, w)
+    own1 = lax.all_to_all(theirs, "x", 0, 0, tiled=True)
+    own2 = lax.all_to_all(after(mine, own1), "x", 0, 0, tiled=True)
+
+    theirs = terms(60, w, own1, *[swap(part, "c", 2) for part in jnp.split(own1, 2)])
     got = swap(theirs, "l", 4)
-    other2 = swap(own2, "c", 2)
-    mine = terms(20, own2, other2, w)
+    own2 = after(own2, theirs)
+    mine = terms(20, w, own2, swap(own2, "c", 2))
     return call(functools.partial(finish_kernel, half_index), (256, 1024), mine, got)
 
 

time: 136 us -> 138 us (1.015)
  blocking collectives: 73.9 us -> 81.6 us
  starting transfers between devices: 19.6 us -> 16.3 us
  waiting for transfers between devices: 9.91 us -> 7.58 us
    all_to_all x2 -> x3, blocking collectives: 44.7 us -> 52.4 us  [the longest x1 20.3 us: shards(): q = lax.all_to_all(q, ('h', 'l'), 0, 0, tiled=True)]
    all_to_all x1, waiting for transfers between devices: 4.8 us -> 0.01 us  [shards(): own2 = lax.all_to_all(after(mine, own1), 'x', 0, 0, tiled=True)]
    ppermute x3 -> x4, starting transfers between devices: 16.1 us -> 12.8 us  [swap(): return lax.ppermute(x, axis, [(i, i ^ 1) for i in range(n)])]
    ppermute x3 -> x4, waiting for transfers between devices: 4.4 us -> 7.56 us  [swap(): return lax.ppermute(x, axis, [(i, i ^ 1) for i in range(n)])]
    unnamed x8 -> x12, local copies, waits for them, and re-layouts: 4.03 us -> 3.98 us
  transfers between devices with their start and end apart: 5 -> 6, of which waited for: 3 -> 3; matrix products, arithmetic and copies ran while one was open for 0% -> 0% of each run, Pallas kernels for 8% -> 8%
where the time goes in v4:
time: 138 us; the launch traced here: 137 us
  blocking collectives  81.6 us (59%)
  starting transfers between devices  16.3 us (12%)
  Pallas kernels  14.3 us (10%)
  between operations  13.5 us (10%)
  waiting for transfers between devices  7.58 us (5%)
  local copies, waits for them, and re-layouts  4.06 us (3%)
    all_to_all x1, blocking collectives, shards(): r = lax.all_to_all(r, ('h', 'x', 'c', 'l'), 0, 0, tiled=True)  29.2 us
    all_to_all x1, blocking collectives, shards(): q = lax.all_to_all(q, ('h', 'l'), 0, 0, tiled=True)  20.3 us
    all_to_all x1, blocking collectives, shards(): q = lax.all_to_all(after(q, r), 'z', 0, 0, tiled=True)  17.6 us
    all_to_all x1, blocking collectives, shards(): own1 = lax.all_to_all(theirs, 'x', 0, 0, tiled=True)  14.4 us
    ppermute x4, starting transfers between devices, swap(): return lax.ppermute(x, axis, [(i, i ^ 1) for i in range(n)])  12.8 us
    pallas_call x2, Pallas kernels, terms(): pl.pallas_call(terms_kernel, in_specs=[far] * (1 + len(left)), out_specs=...  10 us
    ppermute x4, waiting for transfers between devices, swap(): return lax.ppermute(x, axis, [(i, i ^ 1) for i in range(n)])  7.56 us
    pallas_call x5, Pallas kernels, call(): pl.pallas_call(kernel, in_specs=[spec] * len(ops), out_specs=[spec] * out...  4.22 us
  transfers between devices with their start and end apart: 6, of which 3 were waited for; matrix products, arithmetic and copies ran while one was open for 0% of the time, Pallas kernels for 8%

profile of v4, /device:TPU:1, one launch (start us, length us, event | category | flops | bytes accessed | tf_op | source)
XLA Modules:
  0.0 137.3 jit_solution(12526951287126379765)
XLA Ops:
  6.5 0.0 copy-start
  6.5 0.0 all-gather.2.cloned.1.call-start
  6.5 0.0 copy-start.2
  6.5 1.0 copy-done.2
  7.5 0.1 shard_map.30
  7.7 29.2 %all_to_all.25.in_ref = f32[64,16,128]{2,1,0:T(8,128)S(1)} all-to-all(f32[64,16,128]{2,1,0:T(8,128)S(1)} %shard_map.30), channel_id=1, replica_groups=mesh['z'=8,'h'=2,'x'=4,'c'=2,'l'=4] {'h','x','c','l'}, dimensions={0} | all-to-all | bytes 1048576 | tf_op jit(solution)/shard_map/all_to_all | solution.py:200
  36.8 1.4 %shard_map.31 = f32[2,4,2,16,512]{4,3,2,1,0:T(8,128)} custom-call(f32[64,16,128]{2,1,0:T(8,128)S(1)} %all_to_all.25.in_ref), custom_call_target="tpu_custom_call" | custom-call | bytes 1048576 | tf_op jit(solution)/shard_map/pallas_call | solution.py:179
  38.2 0.0 all-gather.2.cloned.1.call-update
  38.3 0.0 copy-done
  38.3 17.6 %all_to_all.26.in_ref = f32[8,32,128]{2,1,0:T(8,128)S(1)} all-to-all(f32[8,32,128]{2,1,0:T(8,128)S(1)} %bitcast_bitcast_fusion), channel_id=1, replica_groups=mesh['z'=8,'h'=2,'x'=4,'c'=2,'l'=4] {'z'}, dimensions={0} | all-to-all | bytes 262144 | tf_op jit(solution)/shard_map/all_to_all | solution.py:205
  55.9 0.1 shard_map.28
  56.0 20.3 %all_to_all.27.in_ref = f32[8,8,16,128]{3,2,1,0:T(8,128)S(1)} all-to-all(f32[8,8,16,128]{3,2,1,0:T(8,128)S(1)} %shard_map.28), channel_id=1, replica_groups=mesh['z'=8,'h'=2,'x'=4,'c'=2,'l'=4] {'h','l'}, dimensions={0} | all-to-all | bytes 1048576 | tf_op jit(solution)/shard_map/all_to_all | solution.py:207
  76.4 1.3 shard_map.29
  77.7 14.4 %all_to_all.28.refs_0_ = f32[4,2,256,128]{3,2,1,0:T(8,128)S(1)} all-to-all(f32[4,2,256,128]{3,2,1,0:T(8,128)S(1)} %get-tuple-element.10), channel_id=1, replica_groups=mesh['z'=8,'h'=2,'x'=4,'c'=2,'l'=4] {'x'}, dimensions={0} | all-to-all | bytes 2097152 | tf_op jit(solution)/shard_map/all_to_all | solution.py:209
  92.1 0.0 copy-start.3
  92.1 3.5 %all-to-all-start.3 = ((f32[4,2,256,128]{3,2,1,0:T(8,128)}), f32[4,2,256,128]{3,2,1,0:T(8,128)S(1)}, u32[]{:S(2)}, u32[]{:S(2)}) async-start(f32[4,2,256,128]{3,2,1,0:T(8,128)} %get-tuple-element.11), calls=%async_computation.3 | async-start | bytes 2097152 | tf_op jit(solution)/shard_map/all_to_all | solution.py:210
  95.7 0.1 fusion
  95.7 5.9 %collective-permute-start = (f32[2,2,256,128]{3,2,1,0:T(8,128)S(1)}, f32[2,2,256,128]{3,2,1,0:T(8,128)S(1)}, u32[]{:S(2)}, u32[]{:S(2)}) collective-permute-start(f32[2,2,256,128]{3,2,1,0:T(8,128)S(1)} %get-tuple-element.14), channel_id=1, source_target_pairs={{0,4},{4,0},{1,5},{5,1},{2,6},{6,2},{3,7},{7,3},{8,12},{12,8},{9,1... | collective-permute-start | bytes 1572872 | tf_op jit(solution)/shard_map/ppermute | solution.py:194
  101.7 1.9 %collective-permute-start.1 = (f32[2,2,256,128]{3,2,1,0:T(8,128)S(1)}, f32[2,2,256,128]{3,2,1,0:T(8,128)S(1)}, u32[]{:S(2)}, u32[]{:S(2)}) collective-permute-start(f32[2,2,256,128]{3,2,1,0:T(8,128)S(1)} %get-tuple-element.13), channel_id=1, source_target_pairs={{0,4},{4,0},{1,5},{5,1},{2,6},{6,2},{3,7},{7,3},{8,12},{12,8},{9,1... | collective-permute-start | bytes 1572872 | tf_op jit(solution)/shard_map/ppermute | solution.py:194
  103.6 0.0 collective-permute-done.refs_1_
  103.6 0.0 copy-start.4
  103.6 1.9 %collective-permute-done.1.refs_2_ = f32[2,2,256,128]{3,2,1,0:T(8,128)S(1)} collective-permute-done((f32[2,2,256,128]{3,2,1,0:T(8,128)S(1)}, f32[2,2,256,128]{3,2,1,0:T(8,128)S(1)}, u32[]{:S(2)}, u32[]{:S(2)}) %collective-permute-start.1) | collective-permute-done | bytes 524320 | tf_op jit(solution)/shard_map/ppermute | solution.py:194
  105.5 0.0 copy-start.5
  105.5 0.0 all-gather.2.cloned.1.call-done.refs_3_.refs_2_
  105.5 0.0 copy-done.3
  105.5 0.0 copy-done.4
  105.5 0.8 copy-done.5
  106.3 4.5 %shard_map.32 = f32[256,512]{1,0:T(8,128)} custom-call(f32[4,2,256,128]{3,2,1,0:T(8,128)} %copy-done.3, f32[2,2,256,128]{3,2,1,0:T(8,128)} %copy-done.4, f32[2,2,256,128]{3,2,1,0:T(8,128)} %copy-done.5, f32[8,2,128,512]{3,2,1,0:T(8,128)} %all-gather.2.cloned.1.call-done.refs_3_.refs_2_), custom_call_target="tpu_custom_call" | custom-call | flops 1610612736 | bytes 6291456 | tf_op jit(solution)/shard_map/pallas_call | solution.py:143
  110.8 0.0 all-to-all-done.3.refs_0_
  110.8 2.8 %collective-permute-start.2 = (f32[4,2,256,128]{3,2,1,0:T(8,128)S(1)}, f32[4,2,256,128]{3,2,1,0:T(8,128)S(1)}, u32[]{:S(2)}, u32[]{:S(2)}) collective-permute-start(f32[4,2,256,128]{3,2,1,0:T(8,128)S(1)} %all-to-all-done.3.refs_0_), channel_id=1, source_target_pairs={{0,4},{4,0},{1,5},{5,1},{2,6},{6,2},{3,7},{7,3},{8,12},{12,8},{9,1... | collective-permute-start | bytes 3145736 | tf_op jit(solution)/shard_map/ppermute | solution.py:194
  113.6 2.2 %collective-permute-start.3 = (f32[256,512]{1,0:T(8,128)}, f32[256,512]{1,0:T(8,128)S(1)}, u32[]{:S(2)}, u32[]{:S(2)}) collective-permute-start(f32[256,512]{1,0:T(8,128)} %shard_map.32), channel_id=1, source_target_pairs={{0,1},{1,0},{2,3},{3,2},{4,5},{5,4},{6,7},{7,6},{8,9},{9,8},{10,11... | collective-permute-start | bytes 1572872 | tf_op jit(solution)/shard_map/ppermute | solution.py:194
  115.8 0.1 collective-permute-done.2.refs_1_
  115.9 0.0 copy-start.1
  115.9 2.2 %copy-done.1 = f32[8,2,128,512]{3,2,1,0:T(8,128)S(1)} copy-done((f32[8,2,128,512]{3,2,1,0:T(8,128)S(1)}, f32[8,2,128,512]{3,2,1,0:T(8,128)}, u32[]{:S(2)}) %copy-start.1) | copy-done | bytes 4194328
  118.0 5.6 %shard_map.33.mine_ref = f32[256,512]{1,0:T(8,128)S(1)} custom-call(f32[4,2,256,128]{3,2,1,0:T(8,128)S(1)} %all-to-all-done.3.refs_0_, f32[4,2,256,128]{3,2,1,0:T(8,128)S(1)} %collective-permute-done.2.refs_1_, f32[8,2,128,512]{3,2,1,0:T(8,128)S(1)} %copy-done.1), custom_call_target="tpu_custom_call" | custom-call | flops 1610612736 | bytes 6291456 | tf_op jit(solution)/shard_map/pallas_call | solution.py:143
  123.6 5.6 %collective-permute-done.3.got_ref = f32[256,512]{1,0:T(8,128)S(1)} collective-permute-done((f32[256,512]{1,0:T(8,128)}, f32[256,512]{1,0:T(8,128)S(1)}, u32[]{:S(2)}, u32[]{:S(2)}) %collective-permute-start.3) | collective-permute-done | bytes 524320 | tf_op jit(solution)/shard_map/ppermute | solution.py:194
  129.2 1.2 shard_map.34
  (1 shorter events, 0.0 us)
Async XLA Ops:
  6.5 31.7 %copy-start = (f32[32,1024]{1,0:T(8,128)S(1)}, f32[32,1024]{1,0:T(8,128)}, u32[]{:S(2)}) copy-start(f32[32,1024]{1,0:T(8,128)} %param.2) | copy-start | bytes 393220
  6.5 98.9 %all-gather.2.cloned.1.call-start = ((), (), s32[]{:S(2)}) async-start(), calls=%async_computation.5 | async-start | bytes 4718592 | tf_op jit(solution)/shard_map/all_gather | solution.py:203
  6.5 1.0 copy-start.2
  92.1 13.3 %copy-start.3 = (f32[4,2,256,128]{3,2,1,0:T(8,128)}, f32[4,2,256,128]{3,2,1,0:T(8,128)S(1)}, u32[]{:S(2)}) copy-start(f32[4,2,256,128]{3,2,1,0:T(8,128)S(1)} %all_to_all.28.refs_0_) | copy-start | bytes 3145732
  92.1 18.6 %all-to-all-start.3 = ((f32[4,2,256,128]{3,2,1,0:T(8,128)}), f32[4,2,256,128]{3,2,1,0:T(8,128)S(1)}, u32[]{:S(2)}, u32[]{:S(2)}) async-start(f32[4,2,256,128]{3,2,1,0:T(8,128)} %get-tuple-element.11), calls=%async_computation.3 | async-start | bytes 2097152 | tf_op jit(solution)/shard_map/all_to_all | solution.py:210
  95.7 7.9 %collective-permute-start = (f32[2,2,256,128]{3,2,1,0:T(8,128)S(1)}, f32[2,2,256,128]{3,2,1,0:T(8,128)S(1)}, u32[]{:S(2)}, u32[]{:S(2)}) collective-permute-start(f32[2,2,256,128]{3,2,1,0:T(8,128)S(1)} %get-tuple-element.14), channel_id=1, source_target_pairs={{0,4},{4,0},{1,5},{5,1},{2,6},{6,2},{3,7},{7,3},{8,12},{12,8},{9,1... | collective-permute-start | bytes 1572872 | tf_op jit(solution)/shard_map/ppermute | solution.py:194
  101.7 3.8 %collective-permute-start.1 = (f32[2,2,256,128]{3,2,1,0:T(8,128)S(1)}, f32[2,2,256,128]{3,2,1,0:T(8,128)S(1)}, u32[]{:S(2)}, u32[]{:S(2)}) collective-permute-start(f32[2,2,256,128]{3,2,1,0:T(8,128)S(1)} %get-tuple-element.13), channel_id=1, source_target_pairs={{0,4},{4,0},{1,5},{5,1},{2,6},{6,2},{3,7},{7,3},{8,12},{12,8},{9,1... | collective-permute-start | bytes 1572872 | tf_op jit(solution)/shard_map/ppermute | solution.py:194
  103.6 1.9 %copy-start.4 = (f32[2,2,256,128]{3,2,1,0:T(8,128)}, f32[2,2,256,128]{3,2,1,0:T(8,128)S(1)}, u32[]{:S(2)}) copy-start(f32[2,2,256,128]{3,2,1,0:T(8,128)S(1)} %collective-permute-done.refs_1_) | copy-start | bytes 1572868
  105.5 0.8 copy-start.5
  110.8 5.1 %collective-permute-start.2 = (f32[4,2,256,128]{3,2,1,0:T(8,128)S(1)}, f32[4,2,256,128]{3,2,1,0:T(8,128)S(1)}, u32[]{:S(2)}, u32[]{:S(2)}) collective-permute-start(f32[4,2,256,128]{3,2,1,0:T(8,128)S(1)} %all-to-all-done.3.refs_0_), channel_id=1, source_target_pairs={{0,4},{4,0},{1,5},{5,1},{2,6},{6,2},{3,7},{7,3},{8,12},{12,8},{9,1... | collective-permute-start | bytes 3145736 | tf_op jit(solution)/shard_map/ppermute | solution.py:194
  113.6 15.6 %collective-permute-start.3 = (f32[256,512]{1,0:T(8,128)}, f32[256,512]{1,0:T(8,128)S(1)}, u32[]{:S(2)}, u32[]{:S(2)}) collective-permute-start(f32[256,512]{1,0:T(8,128)} %shard_map.32), channel_id=1, source_target_pairs={{0,1},{1,0},{2,3},{3,2},{4,5},{5,4},{6,7},{7,6},{8,9},{9,8},{10,11... | collective-permute-start | bytes 1572872 | tf_op jit(solution)/shard_map/ppermute | solution.py:194
  115.9 2.2 %copy-start.1 = (f32[8,2,128,512]{3,2,1,0:T(8,128)S(1)}, f32[8,2,128,512]{3,2,1,0:T(8,128)}, u32[]{:S(2)}) copy-start(f32[8,2,128,512]{3,2,1,0:T(8,128)} %all-gather.2.cloned.1.call-done.refs_3_.refs_2_) | copy-start | bytes 12582916
Sparse Core Ops, SparseCore 0:
  38.4 58.0 all-gather.1
